TPU v7x, 32 devices: a whole 2x2x4 slice. The times are simulated.
32 devices in a mesh: fsdp: 8 (over z, core), ctx: 4 (over y, x).
Axes of the slice: x: 2, y: 2, z: 4, core: 2. Of those that a mesh axis runs over, the one named last changes fastest.
Arguments:
- tokens: bfloat16 [8, 4096, 1088], P('fsdp', 'ctx'), may hold values from -6 to 6
- cotangent: bfloat16 [8, 4096, 1088], P('fsdp', 'ctx'), may hold values from -6 to 6
- lengths: int32 [8], P('fsdp'), may hold values from 1024 to 4096, as said below
- block_order: int32 [8, 8], P('fsdp'), may hold values from 0 to 7, each once within a row
- ln1_gain: float32 [2, 1088], P(None, 'fsdp'), may hold values from 0.25 to 1.75
- ln1_bias: float32 [2, 1088], P(None, 'fsdp'), may hold values from -1 to 1
- qkv_weight: float32 [2, 1088, 3264], P(None, 'fsdp'), may hold values from -0.1875 to 0.1875
- q_bias: float32 [2, 1088], P(None, 'fsdp'), may hold values from -1.5 to 1.5
- v_bias: float32 [2, 1088], P(None, 'fsdp'), may hold values from -1.5 to 1.5
- out_weight: float32 [2, 1088, 1088], P(None, 'fsdp'), may hold values from -1.5 to 1.5
- out_bias: float32 [2, 1088], P(None, 'fsdp'), may hold values from -1 to 1
- ln2_gain: float32 [2, 1088], P(None, 'fsdp'), may hold values from 0.25 to 1.75
- ln2_bias: float32 [2, 1088], P(None, 'fsdp'), may hold values from -1 to 1
- up_weight: float32 [2, 1088, 4352], P(None, 'fsdp'), may hold values from -0.1875 to 0.1875
- up_bias: float32 [2, 4352], P(None, 'fsdp'), may hold values from -1.5 to 1.5
- down_weight: float32 [2, 4352, 1088], P(None, 'fsdp'), may hold values from -0.09375 to 0.09375
- down_bias: float32 [2, 1088], P(None, 'fsdp'), may hold values from -1 to 1
Outputs:
- activations: bfloat16 [8, 4096, 1088], P('fsdp', 'ctx')
- tokens_grad: float32 [8, 4096, 1088], P('fsdp', 'ctx')
- ln1_gain_grad: float32 [2, 1088], P(None, 'fsdp')
- ln1_bias_grad: float32 [2, 1088], P(None, 'fsdp')
- qkv_weight_grad: float32 [2, 1088, 3264], P(None, 'fsdp')
- q_bias_grad: float32 [2, 1088], P(None, 'fsdp')
- v_bias_grad: float32 [2, 1088], P(None, 'fsdp')
- out_weight_grad: float32 [2, 1088, 1088], P(None, 'fsdp')
- out_bias_grad: float32 [2, 1088], P(None, 'fsdp')
- ln2_gain_grad: float32 [2, 1088], P(None, 'fsdp')
- ln2_bias_grad: float32 [2, 1088], P(None, 'fsdp')
- up_weight_grad: float32 [2, 1088, 4352], P(None, 'fsdp')
- up_bias_grad: float32 [2, 4352], P(None, 'fsdp')
- down_weight_grad: float32 [2, 4352, 1088], P(None, 'fsdp')
- down_bias_grad: float32 [2, 1088], P(None, 'fsdp')
Inputs may be any that keep to these rules, and one draw needn't show every extreme that they name: Some slot holds exactly 4096 valid tokens and some exactly 1024; valid tokens are the first lengths of the sequence positions. `block_order`: each row names every block of its slot once.
All inputs are finite; a program needn't handle non-finite values.
Results may differ from a plain program's by a relative error of at most 0.019.
Values may be sent and summed in bfloat16 or wider, within the bound.
A program may use at most 512 MiB of HBM per device.

v0:
```python
import functools
import jax, jax.numpy as jnp
from jax import lax
from jax.experimental import pallas as pl
from jax.experimental.pallas import tpu as pltpu
from jax.experimental.layout import Layout, with_layout_constraint
from jax.sharding import Mesh, PartitionSpec as P
f32=jnp.float32; bf16=jnp.bfloat16
NEG=-1e30
def dot_nt(a,b): return lax.dot_general(a,b,(((1,),(1,)),((),())),preferred_element_type=f32)
def dot_nn(a,b): return lax.dot_general(a,b,(((1,),(0,)),((),())),preferred_element_type=f32)

LOG2E=1.4426950408889634
def split(q,h,low):
    qs=q.astype(f32)*(0.125*LOG2E)
    hi=qs.astype(bf16).astype(f32); lo=qs-hi
    rl=pltpu.roll(lo,64,1)
    c=jnp.where(low,hi,rl) if h==0 else jnp.where(low,rl,hi)
    return c.astype(bf16)
def dup(k,h,low):
    kf=k.astype(f32); rl=pltpu.roll(kf,64,1)
    c=jnp.where(low,kf,rl) if h==0 else jnp.where(low,rl,kf)
    return c.astype(bf16)
def fwd_kernel(inv_ref, nb_ref, x_ref, o_ref, lse_ref, vt, kd, sb, acc, *, B, NB):
    s=pl.program_id(0)
    nb=nb_ref[s]
    lane=lax.broadcasted_iota(jnp.int32,(1,128),1)
    low=lane<64
    def tv(j,_):
        r=pl.multiple_of(inv_ref[s,j]*B,B)
        w=pl.multiple_of(j*B,B)
        t=x_ref[0,pl.ds(r,B),256:384].T
        one=(lax.broadcasted_iota(jnp.int32,(16,B),0)==0).astype(bf16)
        for h in range(2):
            vt[80*h:80*h+64,pl.ds(w,B)]=t[64*h:64*h+64,:]
            vt[80*h+64:80*h+80,pl.ds(w,B)]=one
            kd[h,pl.ds(w,B),:]=dup(x_ref[0,pl.ds(r,B),128:256],h,low)
        return 0
    lax.fori_loop(0,nb,tv,0)
    rr=lax.broadcasted_iota(jnp.int32,(B,B),0)
    cc=lax.broadcasted_iota(jnp.int32,(B,B),1)
    def qblock(i,_):
        r=pl.multiple_of(inv_ref[s,i]*B,B)
        q=x_ref[0,pl.ds(r,B),0:128]
        qh=[split(q,h,low) for h in range(2)]
        acc[...]=jnp.zeros_like(acc)
        def scores(j,slot):
            for h in range(2):
                sb[slot,h]=dot_nt(kd[h,pl.ds(pl.multiple_of(j*B,B),B),:],qh[h])
        def step(j,carry,diag):
            out=[]
            for h in range(2):
                m=carry[h]
                st=sb[j%2,h]
                if diag: st=jnp.where(rr<=cc,st,NEG)
                mn=jnp.maximum(m,jnp.max(st,axis=0,keepdims=True))
                p=jnp.exp2(st-mn)
                al=jnp.exp2(m-mn)
                v=vt[80*h:80*h+80,pl.ds(pl.multiple_of(j*B,B),B)]
                acc[h]=acc[h]*al+dot_nn(v,p.astype(bf16))
                out.append(mn)
            return tuple(out)
        scores(0,0)
        def both(j,c):
            scores(j+1,(j+1)%2)
            return step(j,c,False)
        n=jnp.full((1,B),NEG,f32)
        c=lax.fori_loop(0,i,both,(n,n))
        c=step(i,c,True)
        os=[]
        for h in range(2):
            l=acc[h,64:65,:]
            os.append(acc[h,0:64,:]*(1.0/l))
            lse_ref[0,pl.ds(h,1),pl.ds(r,B)]=c[h]+jnp.log2(l)
        o_ref[0,pl.ds(r,B),:]=jnp.concatenate(os,0).T.astype(bf16)
        return 0
    lax.fori_loop(0,nb,qblock,0)
    def pad(i,_):
        r=pl.multiple_of(inv_ref[s,i]*B,B)
        o_ref[0,pl.ds(r,B),:]=jnp.zeros((B,128),bf16)
        lse_ref[0,:,pl.ds(r,B)]=jnp.zeros((8,B),f32)
        return 0
    lax.fori_loop(nb,NB,pad,0)

def flash_fwd(x,inv,nb,B):
    S,N,_=x.shape
    NB=N//B
    return pl.pallas_call(functools.partial(fwd_kernel,B=B,NB=NB),
      out_shape=(jax.ShapeDtypeStruct((S,N,128),bf16),jax.ShapeDtypeStruct((S,8,N),f32)),
      grid_spec=pltpu.PrefetchScalarGridSpec(num_scalar_prefetch=2,grid=(S,),
        in_specs=[pl.BlockSpec((1,N,384),lambda s,*_:(s,0,0))],
        out_specs=[pl.BlockSpec((1,N,128),lambda s,*_:(s,0,0)),pl.BlockSpec((1,8,N),lambda s,*_:(s,0,0))],
        scratch_shapes=[pltpu.VMEM((160,N),bf16),pltpu.VMEM((2,N,128),bf16),pltpu.VMEM((2,2,B,B),f32),pltpu.VMEM((2,80,B),f32)]),
      compiler_params=pltpu.CompilerParams(vmem_limit_bytes=48<<20),
      cost_estimate=pl.CostEstimate(flops=S*4*N*N*128,bytes_accessed=S*N*1024,transcendentals=S*N*N),
      )(inv,nb,x)

def bwd_kernel(inv_ref, nb_ref, x_ref, o_ref, do_ref, lse_ref, dx_ref, kt, qd, dq, dk, dv, dl, *, B, NB):
    s=pl.program_id(0)
    nb=nb_ref[s]
    lane=lax.broadcasted_iota(jnp.int32,(1,128),1)
    low=lane<64
    hm=(lax.broadcasted_iota(jnp.int32,(8,128),1)//64==lax.broadcasted_iota(jnp.int32,(8,128),0)).astype(bf16)
    def prep(j,_):
        r=pl.multiple_of(inv_ref[s,j]*B,B)
        w=pl.multiple_of(j*B,B)
        kt[:,pl.ds(w,B)]=x_ref[0,pl.ds(r,B),128:256].T
        for h in range(2): qd[h,pl.ds(w,B),:]=split(x_ref[0,pl.ds(r,B),0:128],h,low)
        prod=o_ref[0,pl.ds(r,B),:].astype(f32)*do_ref[0,pl.ds(r,B),:].astype(f32)
        hi=prod.astype(bf16); lo=(prod-hi.astype(f32)).astype(bf16)
        dl[:,pl.ds(w,B)]=dot_nt(hm,hi)+dot_nt(hm,lo)
        dq[:,pl.ds(w,B)]=jnp.zeros((128,B),f32)
        return 0
    lax.fori_loop(0,nb,prep,0)
    rr=lax.broadcasted_iota(jnp.int32,(B,B),0)
    cc=lax.broadcasted_iota(jnp.int32,(B,B),1)
    def kblock(j,_):
        r=pl.multiple_of(inv_ref[s,j]*B,B)
        k=x_ref[0,pl.ds(r,B),128:256]
        v=x_ref[0,pl.ds(r,B),256:384]
        kdh=[dup(k,h,low) for h in range(2)]
        dk[...]=jnp.zeros_like(dk); dv[...]=jnp.zeros_like(dv)
        def step(i,diag):
            ri=pl.multiple_of(inv_ref[s,i]*B,B)
            wi=pl.multiple_of(i*B,B)
            q=x_ref[0,pl.ds(ri,B),0:128]*jnp.asarray(0.125,bf16)
            do=do_ref[0,pl.ds(ri,B),:]
            zero=jnp.zeros_like(q)
            dvs=[];dks=[]
            for h in range(2):
                qh=jnp.where(low,q,zero) if h==0 else jnp.where(low,zero,q)
                doh=jnp.where(low,do,zero) if h==0 else jnp.where(low,zero,do)
                st=dot_nt(kdh[h],qd[h,pl.ds(wi,B),:])
                p=jnp.exp2(st-lse_ref[0,pl.ds(h,1),pl.ds(ri,B)])
                if diag: p=jnp.where(rr<=cc,p,0.0)
                dvs.append(dot_nn(p.astype(bf16),doh))
                dp=dot_nt(v,doh)
                ds=(p*(dp-dl[pl.ds(h,1),pl.ds(wi,B)])).astype(bf16)
                dks.append(dot_nn(ds,qh))
                kh=kt[64*h:64*h+64,pl.ds(pl.multiple_of(j*B,B),B)]
                dq[64*h:64*h+64,pl.ds(wi,B)]+=dot_nn(kh,ds)
            dv[...]+=dvs[0]+dvs[1]
            dk[...]+=dks[0]+dks[1]
        step(j,True)
        def body(i,_):
            step(i,False); return 0
        lax.fori_loop(j+1,nb,body,0)
        dx_ref[0,pl.ds(r,B),128:256]=dk[...].astype(bf16)
        dx_ref[0,pl.ds(r,B),256:384]=dv[...].astype(bf16)
        return 0
    lax.fori_loop(0,nb,kblock,0)
    def fin(i,_):
        r=pl.multiple_of(inv_ref[s,i]*B,B)
        dx_ref[0,pl.ds(r,B),0:128]=(dq[:,pl.ds(pl.multiple_of(i*B,B),B)].T*0.125).astype(bf16)
        return 0
    lax.fori_loop(0,nb,fin,0)
    def pad(i,_):
        r=pl.multiple_of(inv_ref[s,i]*B,B)
        dx_ref[0,pl.ds(r,B),:]=jnp.zeros((B,384),bf16)
        return 0
    lax.fori_loop(nb,NB,pad,0)

def flash_bwd(x,o,do,lse,inv,nb,B):
    S,N,_=x.shape
    NB=N//B
    return pl.pallas_call(functools.partial(bwd_kernel,B=B,NB=NB),
      out_shape=jax.ShapeDtypeStruct((S,N,384),bf16),
      grid_spec=pltpu.PrefetchScalarGridSpec(num_scalar_prefetch=2,grid=(S,),
        in_specs=[pl.BlockSpec((1,N,384),lambda s,*_:(s,0,0)),pl.BlockSpec((1,N,128),lambda s,*_:(s,0,0)),
                  pl.BlockSpec((1,N,128),lambda s,*_:(s,0,0)),pl.BlockSpec((1,8,N),lambda s,*_:(s,0,0))],
        out_specs=pl.BlockSpec((1,N,384),lambda s,*_:(s,0,0)),
        scratch_shapes=[pltpu.VMEM((128,N),bf16),pltpu.VMEM((2,N,128),bf16),pltpu.VMEM((128,N),f32),pltpu.VMEM((B,128),f32),pltpu.VMEM((B,128),f32),pltpu.VMEM((8,N),f32)]),
      compiler_params=pltpu.CompilerParams(vmem_limit_bytes=48<<20),
      cost_estimate=pl.CostEstimate(flops=S*10*N*N*128,bytes_accessed=S*N*2400,transcendentals=S*N*N),
      )(inv,nb,x,o,do,lse)


def one_fwd_kernel(own_ref, q_ref, x_ref, o_ref, lse_ref, vt, sb, acc, *, B, NB):
    nb = own_ref[NB + 2]
    def tv(j,_):
        r=pl.multiple_of(own_ref[j]*B,B)
        t=x_ref[pl.ds(r,B),:].T
        w=pl.multiple_of(j*B,B)
        vt[0:64,pl.ds(w,B)]=t[64:128,:]
        vt[64:80,pl.ds(w,B)]=(lax.broadcasted_iota(jnp.int32,(16,B),0)==0).astype(bf16)
        return 0
    lax.fori_loop(0,nb,tv,0)
    rr=lax.broadcasted_iota(jnp.int32,(B,B),0)
    cc=lax.broadcasted_iota(jnp.int32,(B,B),1)
    for t in range(2):
        i=own_ref[NB+t]
        @pl.when(i>=nb)
        def _():
            o_ref[t*B:(t+1)*B,:]=jnp.zeros((B,64),bf16)
            lse_ref[:,t*B:(t+1)*B]=jnp.zeros((8,B),f32)
        @pl.when(i<nb)
        def _():
            qs=q_ref[t*B:(t+1)*B,:].astype(f32)*(0.125*LOG2E)
            q=qs.astype(bf16)
            ql=(qs-q.astype(f32)).astype(bf16)
            acc[...]=jnp.zeros_like(acc)
            def step(j,m,diag):
                k=x_ref[pl.ds(pl.multiple_of(own_ref[j]*B,B),B),0:64]
                st=dot_nt(k,q)+dot_nt(k,ql)
                if diag: st=jnp.where(rr<=cc,st,NEG)
                mn=jnp.maximum(m,jnp.max(st,axis=0,keepdims=True))
                p=jnp.exp2(st-mn)
                al=jnp.exp2(m-mn)
                v=vt[:,pl.ds(pl.multiple_of(j*B,B),B)]
                acc[...]=acc[...]*al+dot_nn(v,p.astype(bf16))
                return mn
            m=lax.fori_loop(0,i,lambda j,m: step(j,m,False),jnp.full((1,B),NEG,f32))
            m=step(i,m,True)
            l=acc[64:65,:]
            o_ref[t*B:(t+1)*B,:]=(acc[0:64,:]*(1.0/l)).T.astype(bf16)
            lse_ref[:,t*B:(t+1)*B]=jnp.broadcast_to(m+jnp.log2(l),(8,B))


def one_fwd(q,x,own,B):
    N=x.shape[0]; R=q.shape[0]; NB=N//B
    full=lambda *_:(0,0)
    last=lambda *_:(0,3)
    return pl.pallas_call(functools.partial(one_fwd_kernel,B=B,NB=NB),
      out_shape=(jax.ShapeDtypeStruct((R,64),bf16),jax.ShapeDtypeStruct((8,R),f32)),
      grid_spec=pltpu.PrefetchScalarGridSpec(num_scalar_prefetch=1,grid=(1,),
        in_specs=[pl.BlockSpec((R,64),full),pl.BlockSpec((N,128),last)],
        out_specs=[pl.BlockSpec((R,64),full),pl.BlockSpec((8,R),full)],
        scratch_shapes=[pltpu.VMEM((80,N),bf16),pltpu.VMEM((B,B),f32),pltpu.VMEM((80,B),f32)]),
      compiler_params=pltpu.CompilerParams(vmem_limit_bytes=48<<20),
      cost_estimate=pl.CostEstimate(flops=4*R*N*128,bytes_accessed=N*256+R*512,transcendentals=R*N),
      )(own,q,x)


def one_bwd_kernel(own_ref, q_ref, x_ref, o_ref, do_ref, lse_ref, dq_ref, dx_ref, dkv, dq, *, B, NB):
    nb = own_ref[NB + 2]
    rr=lax.broadcasted_iota(jnp.int32,(B,B),0)
    cc=lax.broadcasted_iota(jnp.int32,(B,B),1)
    ones=jnp.ones((8,64),bf16)
    dkv[...]=jnp.zeros_like(dkv)
    for t in range(2):
        i=own_ref[NB+t]
        sl=slice(t*B,(t+1)*B)
        @pl.when(i>=nb)
        def _():
            dq_ref[sl,:]=jnp.zeros((B,64),bf16)
        @pl.when(i<nb)
        def _():
            qr=q_ref[sl,:]
            qs=qr.astype(f32)*(0.125*LOG2E)
            q=qs.astype(bf16)
            ql=(qs-q.astype(f32)).astype(bf16)
            qd=qr*jnp.asarray(0.125,bf16)
            do=do_ref[sl,:]
            prod=o_ref[sl,:].astype(f32)*do.astype(f32)
            hi=prod.astype(bf16); lo=(prod-hi.astype(f32)).astype(bf16)
            dl=(dot_nt(ones,hi)+dot_nt(ones,lo))[0:1,:]
            lse=lse_ref[0:1,sl]
            dq[...]=jnp.zeros_like(dq)
            def step(j,diag):
                r=pl.multiple_of(own_ref[j]*B,B)
                k=x_ref[pl.ds(r,B),0:64]
                v=x_ref[pl.ds(r,B),64:128]
                st=dot_nt(k,q)+dot_nt(k,ql)
                p=jnp.exp2(st-lse)
                if diag: p=jnp.where(rr<=cc,p,0.0)
                dp=dot_nt(v,do)
                ds=(p*(dp-dl)).astype(bf16)
                dkv[pl.ds(r,B),64:128]+=dot_nn(p.astype(bf16),do)
                dkv[pl.ds(r,B),0:64]+=dot_nn(ds,qd)
                dq[...]+=dot_nn(k.T,ds)
            def body(j,_):
                step(j,False); return 0
            lax.fori_loop(0,i,body,0)
            step(i,True)
            dq_ref[sl,:]=(dq[...].T*0.125).astype(bf16)
    dx_ref[...]=dkv[...].astype(bf16)


def one_bwd(q,x,o,do,lse,own,B):
    N=x.shape[0]; R=q.shape[0]; NB=N//B
    full=lambda *_:(0,0)
    last=lambda *_:(0,3)
    return pl.pallas_call(functools.partial(one_bwd_kernel,B=B,NB=NB),
      out_shape=(jax.ShapeDtypeStruct((R,64),bf16),jax.ShapeDtypeStruct((N,128),bf16)),
      grid_spec=pltpu.PrefetchScalarGridSpec(num_scalar_prefetch=1,grid=(1,),
        in_specs=[pl.BlockSpec((R,64),full),pl.BlockSpec((N,128),last),pl.BlockSpec((R,64),full),pl.BlockSpec((R,64),full),pl.BlockSpec((8,R),full)],
        out_specs=[pl.BlockSpec((R,64),full),pl.BlockSpec((N,128),full)],
        scratch_shapes=[pltpu.VMEM((N,128),f32),pltpu.VMEM((64,B),f32)]),
      compiler_params=pltpu.CompilerParams(vmem_limit_bytes=48<<20),
      cost_estimate=pl.CostEstimate(flops=10*R*N*128,bytes_accessed=N*512+R*1024,transcendentals=R*N),
      )(own,q,x,o,do,lse)


def join_kernel(*refs, count):
    t = pl.program_id(0)
    stacks, tail, out = refs[:-2], refs[-2], refs[-1]
    for i, ref in enumerate(stacks):
        @pl.when((t >= i * count) & (t < (i + 1) * count))
        def _(ref=ref):
            out[...] = ref[0]

    @pl.when(t >= len(stacks) * count)
    def _():
        out[:, :tail.shape[1]] = tail[...]


def join(stacks, tail):
    C, R, W = stacks[0].shape
    n = len(stacks)
    T = tail.shape[1]

    def at(i):
        return lambda t: (jnp.clip(t - i * C, 0, C - 1), 0, 0)
    return pl.pallas_call(functools.partial(join_kernel, count=C),
        out_shape=jax.ShapeDtypeStruct((R, n * C * W + T), bf16),
        grid=(n * C + 1,),
        in_specs=[pl.BlockSpec((1, R, W), at(i)) for i in range(n)] + [pl.BlockSpec((R, T), lambda t: (0, 0))],
        out_specs=pl.BlockSpec((R, W), lambda t: (0, t)),
        compiler_params=pltpu.CompilerParams(vmem_limit_bytes=56 << 20),
        cost_estimate=pl.CostEstimate(flops=0, bytes_accessed=4 * R * (n * C * W + T), transcendentals=0),
    )(*stacks, tail)


def deal_kernel(x_ref, o_ref):
    o_ref[0] = x_ref[...]


def deal(x, first, C, W):
    R = x.shape[0]
    return pl.pallas_call(deal_kernel,
        out_shape=jax.ShapeDtypeStruct((C, R, W), bf16),
        grid=(C,),
        in_specs=[pl.BlockSpec((R, W), lambda t: (0, first + t))],
        out_specs=pl.BlockSpec((1, R, W), lambda t: (t, 0, 0)),
        compiler_params=pltpu.CompilerParams(vmem_limit_bytes=56 << 20),
        cost_estimate=pl.CostEstimate(flops=0, bytes_accessed=4 * R * C * W, transcendentals=0),
    )(x)


def join_kernel(*refs, count):
    t = pl.program_id(0)
    stacks, tail, out = refs[:-2], refs[-2], refs[-1]
    for i, ref in enumerate(stacks):
        @pl.when((t >= i * count) & (t < (i + 1) * count))
        def _(ref=ref):
            out[...] = ref[0]

    @pl.when(t >= len(stacks) * count)
    def _():
        out[:, :tail.shape[1]] = tail[...]


def join(stacks, tail):
    C, R, W = stacks[0].shape
    n = len(stacks)
    T = tail.shape[1]

    def at(i):
        return lambda t: (jnp.clip(t - i * C, 0, C - 1), 0, 0)
    return pl.pallas_call(functools.partial(join_kernel, count=C),
        out_shape=jax.ShapeDtypeStruct((R, n * C * W + T), bf16),
        grid=(n * C + 1,),
        in_specs=[pl.BlockSpec((1, R, W), at(i)) for i in range(n)] + [pl.BlockSpec((R, T), lambda t: (0, 0))],
        out_specs=pl.BlockSpec((R, W), lambda t: (0, t)),
        compiler_params=pltpu.CompilerParams(vmem_limit_bytes=56 << 20),
        cost_estimate=pl.CostEstimate(flops=0, bytes_accessed=4 * R * (n * C * W + T), transcendentals=0),
    )(*stacks, tail)


def deal_kernel(x_ref, o_ref):
    o_ref[0] = x_ref[...]


def deal(x, first, C, W):
    R = x.shape[0]
    return pl.pallas_call(deal_kernel,
        out_shape=jax.ShapeDtypeStruct((C, R, W), bf16),
        grid=(C,),
        in_specs=[pl.BlockSpec((R, W), lambda t: (0, first + t))],
        out_specs=pl.BlockSpec((1, R, W), lambda t: (t, 0, 0)),
        compiler_params=pltpu.CompilerParams(vmem_limit_bytes=56 << 20),
        cost_estimate=pl.CostEstimate(flops=0, bytes_accessed=4 * R * C * W, transcendentals=0),
    )(x)


HEADS = 17
EPSILON = 1e-05
FS = ("zz", "core")


def norm_parts(v):
    mean = jnp.mean(v, axis=-1, keepdims=True)
    c = v - mean
    r = lax.rsqrt(jnp.mean(c * c, axis=-1, keepdims=True) + EPSILON)
    return c * r, r


def norm_back(dn, v, gain):
    xhat, r = norm_parts(v)
    y = dn * gain
    a = jnp.mean(y, axis=-1, keepdims=True)
    b = jnp.mean(y * xhat, axis=-1, keepdims=True)
    return r * (y - a - xhat * b), jnp.sum(dn * xhat, axis=0), jnp.sum(dn, axis=0)


def col_sum(x):
    return jnp.dot(jnp.ones((16, x.shape[0]), bf16), x, preferred_element_type=f32)[0]


def gelu_parts(u):
    z = jnp.abs(u) * 0.7071067811865476
    t = 1.0 / (1.0 + 0.3275911 * z)
    e = jnp.exp(-z * z)
    poly = t * (0.254829592 + t * (-0.284496736 + t * (1.421413741 + t * (-1.453152027 + t * 1.061405429))))
    half = 0.5 * poly * e
    cdf = jnp.where(u >= 0, 1.0 - half, half)
    return u * cdf, cdf + u * e * 0.3989422804014327


def local(
    tokens, cotangent, lengths, block_order,
    ln1_gain, ln1_bias, qkv_weight, q_bias, v_bias, out_weight, out_bias,
    ln2_gain, ln2_bias, up_weight, up_bias, down_weight, down_bias,
    *, G, S,
):
    slots, rows, width = tokens.shape
    C = lax.axis_size("ctx")
    me = lax.axis_index("ctx")
    N = rows * C
    B = rows // 2
    NB = 2 * C
    L = ln1_gain.shape[0]
    shard = ln1_gain.shape[1]
    HW = G * 128
    x_tokens = tokens[0]

    steps = jnp.arange(NB, dtype=jnp.int32)
    order = block_order[0]
    inverse = jnp.sum(jnp.where(order[None, :] == steps[:, None], steps[None, :], 0), axis=1).astype(jnp.int32)
    count = (lengths + (B - 1)) // B
    meta = jnp.concatenate([inverse, count])
    def swap(x):
        return lax.ppermute(x, "core", [(0, 1), (1, 0)])

    metas = [meta, swap(meta)][:S]
    phase_inv = [t[None, :NB] for t in metas]
    phase_nb = [t[NB:] for t in metas]
    own = jnp.concatenate([inverse, lax.dynamic_slice_in_dim(order, 2 * me, 2, 0), count])
    own_pos = (lax.dynamic_slice_in_dim(order, 2 * me, 2, 0)[:, None] * B + jnp.arange(B, dtype=jnp.int32)).reshape(rows, 1)
    live = (own_pos < lengths[0]).astype(f32)

    vectors = [ln1_gain, ln1_bias, q_bias, v_bias, out_bias, ln2_gain, ln2_bias, down_bias, up_bias]
    vec = jnp.concatenate(vectors, axis=1).astype(bf16)
    vec = lax.all_gather(vec, FS).astype(f32)

    def vector(index, layer):
        if index < 8:
            return vec[:, layer, index * shard:(index + 1) * shard].reshape(-1)
        return vec[:, layer, 8 * shard:].reshape(-1)

    def pack(w):
        parts = []
        for g in range(G):
            parts += [w[:, kind * width + g * 128:kind * width + g * 128 + 128] for kind in range(3)]
        last = width - 64
        parts += [w[:, kind * width + last:kind * width + width] for kind in (1, 2, 0)]
        return jnp.concatenate(parts, axis=1)

    def unpack(w):
        tail = G * 384
        parts = []
        for kind, last in enumerate((128, 0, 64)):
            parts += [w[:, g * 384 + kind * 128:g * 384 + kind * 128 + 128] for g in range(G)]
            parts.append(w[:, tail + last:tail + last + 64])
        return jnp.concatenate(parts, axis=1)

    def fetch(w):
        return lax.all_gather(w.astype(bf16), FS, axis=0, tiled=True)

    weights = []
    for layer in range(L):
        weights.append((
            fetch(pack(qkv_weight[layer].astype(bf16))),
            fetch(out_weight[layer]),
            fetch(up_weight[layer]),
            fetch(down_weight[layer]),
        ))

    def plain(x):
        return with_layout_constraint(x, Layout(major_to_minor=tuple(range(x.ndim))))

    def exchange(x):
        return plain(lax.all_to_all(plain(x), "ctx", 0, 0))

    def after(x, *others):
        return lax.optimization_barrier((x,) + others)

    stream = x_tokens.astype(f32)
    records = []
    for layer in range(L):
        qkv_w, out_w, up_w, down_w = weights[layer]
        xhat, _ = norm_parts(stream)
        n1 = (xhat * vector(0, layer) + vector(1, layer)).astype(bf16)
        q_b, v_b = vector(2, layer), vector(3, layer)
        bias = pack(jnp.concatenate([q_b, jnp.zeros_like(q_b), v_b])[None])[0]
        projected = (jnp.dot(n1, qkv_w, preferred_element_type=f32) + bias).astype(bf16)
        wide = [deal(projected, s * C, C, 384) for s in range(S)]
        tail = projected[:, G * 384:]
        if S == 2:
            wide[1] = swap(wide[1])
        kv16 = jnp.broadcast_to(tail[None, :, :128], (C, rows, 128))
        q16 = tail[:, 128:]
        heads, o, lse, o_back = [], [], [], []
        for s in range(S):
            t = wide[s]
            if s == S - 1:
                t = jnp.concatenate([t, kv16], axis=2)
            if s:
                t, heads[0] = after(t, heads[0])
            heads.append(exchange(t).reshape(1, N, -1))
        for s in range(S):
            o_s, lse_s = flash_fwd(heads[s], phase_inv[s], phase_nb[s], B)
            o.append(o_s)
            lse.append(lse_s)
            t = o_s.reshape(C, rows, 128)
            if s:
                t, o_back[0] = after(t, o_back[0])
            o_back.append(exchange(swap(t) if s else t))
        o16, lse16 = one_fwd(q16, heads[-1][0], own, B)
        mixed = join(o_back, o16)
        m = stream + jnp.dot(mixed, out_w, preferred_element_type=f32) + vector(4, layer)
        xhat2, _ = norm_parts(m)
        n2 = (xhat2 * vector(5, layer) + vector(6, layer)).astype(bf16)
        u = jnp.dot(n2, up_w, preferred_element_type=f32) + vector(8, layer)
        a, slope = gelu_parts(u)
        a = a.astype(bf16)
        slope = slope.astype(bf16)
        records.append((stream, n1, heads, q16, o, lse, o16, lse16, mixed, m, n2, a, slope))
        stream = m + jnp.dot(a, down_w, preferred_element_type=f32) + vector(7, layer)
    activations = (stream * live).astype(bf16)[None]

    def reduce_fsdp(g):
        return lax.psum_scatter(g.astype(bf16), FS, scatter_dimension=0, tiled=True)

    def reduce_ctx(g):
        return lax.psum(g, "ctx").astype(f32)

    grad = cotangent[0].astype(f32) * live
    matrices = [None] * L
    fours = [None] * L
    ffns = [None] * L
    small = [None] * L

    def ctx_end(mine):
        return exchange(jnp.broadcast_to(mine[None], (C,) + mine.shape))

    def ctx_sum(shards):
        mine, sizes = ctx_begin(shards)
        return ctx_end(mine), sizes

    def ctx_begin(shards):
        pieces = []
        for t in shards:
            if t.shape[1] == width:
                pieces.append(t.reshape(C, -1, width))
            else:
                pieces.append(jnp.transpose(t.reshape(t.shape[0], C, -1), (1, 0, 2)).reshape(C, -1, width))
        sizes = [t.shape[1] for t in pieces]
        parts = exchange(jnp.concatenate(pieces, axis=1))
        mine = jnp.sum(parts.astype(f32), axis=0).astype(bf16)
        return mine, sizes

    def spread(summed, shapes):
        whole, sizes = summed
        out, at = [], 0
        for n, (r, c) in zip(sizes, shapes):
            t = whole[:, at:at + n].astype(f32)
            at += n
            if c == width:
                out.append(t.reshape(r, c))
            else:
                out.append(jnp.transpose(t.reshape(C, r, c // C), (1, 0, 2)).reshape(r, c))
        return out

    wide_shape, tall_shape = (shard, 4 * width), (4 * shard, width)
    for layer in reversed(range(L)):
        stream_in, n1, heads, q16, o, lse, o16, lse16, mixed, m, n2, a, slope = records[layer]
        qkv_w, out_w, up_w, down_w = weights[layer]
        gb = grad.astype(bf16)
        d_down_b = col_sum(gb)
        d_down = jnp.einsum("rf,rd->fd", a, gb, preferred_element_type=f32).astype(bf16)
        gb, d_down = after(gb, plain(d_down))
        d_down = reduce_fsdp(d_down)
        du = (jnp.einsum("rd,fd->rf", gb, down_w, preferred_element_type=f32) * slope.astype(f32)).astype(bf16)
        d_up_b = col_sum(du)
        d_up = jnp.einsum("rd,rf->df", n2, du, preferred_element_type=f32).astype(bf16)
        du, d_up = after(du, plain(d_up))
        d_up = reduce_fsdp(d_up)
        dn2 = jnp.einsum("rf,df->rd", du, up_w, preferred_element_type=f32)
        back, d_gain2, d_bias2 = norm_back(dn2, m, vector(5, layer))
        gm = grad + back
        gmb = gm.astype(bf16)
        d_out_b = col_sum(gmb)
        d_out = jnp.einsum("rd,re->de", mixed, gmb, preferred_element_type=f32).astype(bf16)
        if layer < L - 1:
            done = after(gmb, *ffn_sum)
            gmb, ffn_sum = done[0], done[1:]
        d_o = []
        for s in range(S):
            w = out_w[C * 128 * s:C * 128 * (s + 1)].reshape(C, 128, width)
            d_o.append(jnp.einsum("re,gce->grc", gmb, w, preferred_element_type=f32).astype(bf16))
        d_o16 = jnp.einsum("re,ce->rc", gmb, out_w[HW:], preferred_element_type=f32).astype(bf16)
        dq16, dkv16 = one_bwd(q16, heads[-1][0], o16, d_o16, lse16, own, B)
        d_oh, d_wide = [], []
        for s in range(S):
            t = d_o[s]
            if s:
                t = swap(t)
            if s == S - 1:
                t = jnp.concatenate([t, dkv16.reshape(C, rows, 128)], axis=2)
            if s:
                t, d_oh[0] = after(t, d_oh[0])
            if s == S - 1 and layer < L - 1:
                t, fours[layer + 1] = after(t, fours[layer + 1])
            d_oh.append(exchange(t).reshape(1, N, -1))
        dkv16 = jnp.sum(d_oh[-1].reshape(C, rows, 256)[:, :, 128:].astype(f32), axis=0)
        for s in range(S):
            t = flash_bwd(heads[s], o[s], d_oh[s], lse[s], phase_inv[s], phase_nb[s], B)
            t = t.reshape(C, rows, 384)
            if s:
                t, d_wide[0], d_down = after(t, d_wide[0], d_down)
            if s == S - 1 and layer < L - 1:
                four_sum = lax.psum((fours[layer + 1], d_down), "ctx")
            d_wide.append(exchange(swap(t) if s else t))
        d_tail = jnp.concatenate([dkv16.astype(bf16), dq16], axis=1)
        d_row = join(d_wide, d_tail)
        d_row, d_up = after(d_row, d_up)
        if layer:
            ffn_sum = lax.psum((d_up, d_down), "ctx")
        else:
            up_sum = ctx_sum([d_up])
        d_qkv = jnp.einsum("rd,rc->dc", n1, d_row, preferred_element_type=f32).astype(bf16)
        d_four = jnp.concatenate([d_qkv, d_out], axis=1)
        if layer:
            d_row, d_four = after(d_row, plain(d_four))
        d_four = reduce_fsdp(d_four)
        sums = unpack(col_sum(d_row)[None])[0]
        dn1 = jnp.einsum("rc,dc->rd", d_row, qkv_w, preferred_element_type=f32)
        back, d_gain1, d_bias1 = norm_back(dn1, stream_in, vector(0, layer))
        grad = gm + back
        fours[layer] = d_four
        ffns[layer] = (d_up, d_down)
        if layer == 0:
            last = ctx_sum([d_four])
            matrices[1] = [four_sum[0].astype(f32), ffn_sum[0].astype(f32), ffn_sum[1].astype(f32)]
            matrices[0] = spread(last, [wide_shape]) + spread(up_sum, [wide_shape]) + [four_sum[1].astype(f32)]
        small[layer] = jnp.concatenate([
            t.reshape(-1, n) for t, n in (
                (d_gain1, shard), (d_bias1, shard), (sums[:width], shard), (sums[2 * width:], shard), (d_out_b, shard),
                (d_gain2, shard), (d_bias2, shard), (d_down_b, shard), (d_up_b, 4 * shard))], axis=1)

    vec_grads = jnp.stack(small, axis=1)
    vec_grads = jnp.sum(lax.all_to_all(vec_grads, FS, 0, 0), axis=0)
    vec_grads = lax.psum(vec_grads, "ctx")
    vg = [vec_grads[:, i * shard:(i + 1) * shard] for i in range(8)] + [vec_grads[:, 8 * shard:]]

    g_qkv = jnp.stack([unpack(matrices[layer][0][:, :3 * width]) for layer in range(L)])
    g_out = jnp.stack([matrices[layer][0][:, 3 * width:] for layer in range(L)])
    g_up = jnp.stack([matrices[layer][1] for layer in range(L)])
    g_down = jnp.stack([matrices[layer][2] for layer in range(L)])
    return (activations, grad[None], vg[0], vg[1], g_qkv, vg[2], vg[3], g_out, vg[4], vg[5], vg[6], g_up, vg[8], g_down, vg[7])


def solution(mesh):
    F, C = mesh.devices.shape
    inner = Mesh(mesh.devices.reshape(F // 2, 2, C), ("zz", "core", "ctx"))
    S = 2 if 16 // (2 * C) >= 2 else 1
    G = S * C
    rows = P(FS, "ctx", None)
    vec, mat = P(None, FS), P(None, FS, None)
    return jax.shard_map(
        functools.partial(local, G=G, S=S),
        mesh=inner,
        in_specs=(rows, rows, P(FS), P(FS, None), vec, vec, mat, vec, vec, mat, vec, vec, vec, mat, vec, mat, vec),
        out_specs=(rows, rows, vec, vec, mat, vec, vec, mat, vec, vec, vec, mat, vec, mat, vec),
        check_vma=False,
    )
```

profile of v0, /device:TPU:0, one launch (start us, length us, event | category | flops | bytes accessed | tf_op | source)
XLA Modules:
  0.0 1561.7 jit_solution(4026493055810497618)
XLA Ops:
  47.6 42.0 %all-gather.15.cloned.1.call-done = bf16[1088,3264]{1,0:T(8,128)(2,1)} async-done(((bf16[136,3264]{1,0:T(8,128)(2,1)}), bf16[1088,3264]{1,0:T(8,128)(2,1)}) %all-gather.15.cloned.1.call-update) | async-done | bytes 7102480 | tf_op jit(solution)/shard_map/all_gather | solution.py:478
  121.8 31.6 %all-to-all-done = bf16[4,1024,384]{2,1,0:T(8,128)(2,1)S(1)} async-done(((bf16[4,1024,384]{2,1,0:T(8,128)(2,1)}), bf16[4,1024,384]{2,1,0:T(8,128)(2,1)S(1)}, u32[]{:S(2)}, u32[]{:S(2)}) %all-to-all-start) | async-done | bytes 3145760 | tf_op jit(solution)/shard_map/all_to_all | solution.py:493
  161.0 32.0 %shard_map.283 = (bf16[1,4096,128]{2,1,0:T(8,128)(2,1)S(1)}, f32[1,8,4096]{2,1,0:T(8,128)S(1)}) custom-call(s32[1,8]{1,0:T(1,128)S(1)} %bitcast.277, s32[1]{0:T(128)S(6)} %select_n.21.nb_ref, bf16[1,4096,384]{2,1,0:T(8,128)(2,1)S(1)} %bitcast.265), custom_call_target="tpu_custom_call" | custom-call | flops 8589934592 | bytes 4194304 | tf_op jit(solution)/shard_map/pallas_call | solution.py:88
  209.3 34.7 %shard_map.282 = (bf16[1,4096,128]{2,1,0:T(8,128)(2,1)S(1)}, f32[1,8,4096]{2,1,0:T(8,128)S(1)}) custom-call(s32[1,8]{1,0:T(1,128)S(1)} %slice_bitcast_fusion.8.inv_ref, s32[1]{0:T(128)} %slice.926.nb_ref, bf16[1,4096,512]{2,1,0:T(8,128)(2,1)} %bitcast.14.x_ref), custom_call_target="tpu_custom_call" | custom-call | flops 8589934592 | bytes 4194304 | tf_op jit(solution)/shard_map/pallas_call | solution.py:88
  282.0 35.4 %multiply_convert_fusion.3 = (bf16[1024,4352]{1,0:T(8,128)(2,1)}, f32[1024,4352]{1,0:T(8,128)}) fusion(f32[4352]{0:T(1024)S(1)} %add.282, bf16[1,1088,4352]{2,1,0:T(8,128)(2,1)} %all-gather.21.cloned.1.call-done, f32[1024,1088]{0,1:T(8,128)} %copy-done.50, f32[1088]{0:T(1024)S(1)} %add.279, f32[1088]{0:T(1024)S(1)} %mul.330, f32[1024]{0:T(1024)S(1)} %add_rsqrt_fusion.2, ...), kind=kOutput, calls=%fused_computation.15 | convolution fusion | flops 9809756160 | bytes 40699392 | tf_op jit(solution)/shard_map/dot_general | solution.py:534
  317.4 18.8 %fusion.141 = (f32[1024]{0:T(1024)S(1)}, f32[1024,1088]{0,1:T(8,128)}) fusion(f32[1088]{0:T(1024)S(1)} %add.291, f32[1024,1088]{0,1:T(8,128)} %copy-done.50, bf16[1024,4352]{1,0:T(8,128)(2,1)} %get-tuple-element.385, bf16[1,4352,1088]{2,1,0:T(8,128)(2,1)} %all-gather.23.cloned.1.call-done), kind=kOutput, calls=%fused_computation.273 | convolution fusion | flops 9700572160 | bytes 27304192 | tf_op jit(solution)/shard_map/dot_general | solution.py:539
  339.1 45.3 %all-gather.17.cloned.1.call-done = bf16[1088,3264]{1,0:T(8,128)(2,1)} async-done(((bf16[136,3264]{1,0:T(8,128)(2,1)}), bf16[1088,3264]{1,0:T(8,128)(2,1)}) %all-gather.17.cloned.1.call-update) | async-done | bytes 7102480 | tf_op jit(solution)/shard_map/all_gather | solution.py:478
  418.2 30.6 %all-to-all-done.4 = bf16[4,1024,384]{2,1,0:T(8,128)(2,1)S(1)} async-done(((bf16[4,1024,384]{2,1,0:T(8,128)(2,1)}), bf16[4,1024,384]{2,1,0:T(8,128)(2,1)S(1)}, u32[]{:S(2)}, u32[]{:S(2)}) %all-to-all-start.4) | async-done | bytes 3145760 | tf_op jit(solution)/shard_map/all_to_all | solution.py:493
  453.7 32.2 %shard_map.289 = (bf16[1,4096,128]{2,1,0:T(8,128)(2,1)S(1)}, f32[1,8,4096]{2,1,0:T(8,128)S(1)}) custom-call(s32[1,8]{1,0:T(1,128)S(1)} %bitcast.278, s32[1]{0:T(128)S(6)} %select_n.21.nb_ref, bf16[1,4096,384]{2,1,0:T(8,128)(2,1)S(1)} %bitcast.267), custom_call_target="tpu_custom_call" | custom-call | flops 8589934592 | bytes 4194304 | tf_op jit(solution)/shard_map/pallas_call | solution.py:88
  504.7 34.6 %shard_map.288 = (bf16[1,4096,128]{2,1,0:T(8,128)(2,1)S(1)}, f32[1,8,4096]{2,1,0:T(8,128)S(1)}) custom-call(s32[1,8]{1,0:T(1,128)S(1)} %slice_bitcast_fusion.8.inv_ref, s32[1]{0:T(128)} %slice.926.nb_ref, bf16[1,4096,512]{2,1,0:T(8,128)(2,1)} %bitcast.25.x_ref), custom_call_target="tpu_custom_call" | custom-call | flops 8589934592 | bytes 4194304 | tf_op jit(solution)/shard_map/pallas_call | solution.py:88
  578.3 35.4 %multiply_convert_fusion.2 = (bf16[1024,4352]{1,0:T(8,128)(2,1)}, f32[1024,4352]{1,0:T(8,128)}) fusion(f32[4352]{0:T(1024)S(1)} %add.309, bf16[1,1088,4352]{2,1,0:T(8,128)(2,1)} %all-gather.27.cloned.1.call-done, f32[1024,1088]{0,1:T(8,128)} %copy-done.39, f32[1088]{0:T(1024)S(1)} %add.306, f32[1088]{0:T(1024)S(1)} %mul.354, f32[1024]{0:T(1024)S(1)} %add_rsqrt_fusion, ...), kind=kOutput, calls=%fused_computation.14 | convolution fusion | flops 9809756160 | bytes 40699392 | tf_op jit(solution)/shard_map/dot_general | solution.py:534
  631.4 31.3 %multiply_convert_fusion.1 = bf16[1024,4352]{1,0:T(8,128)(2,1)} fusion(bf16[1024,1088]{0,1:T(8,128)(2,1)} %fusion.51, bf16[1,4352,1088]{2,1,0:T(8,128)(2,1)} %all-gather.29.cloned.1.call-done, f32[1024,4352]{1,0:T(8,128)} %get-tuple-element.392, f32[4352]{0:T(1024)S(1)} %add.309), kind=kOutput, calls=%fused_computation.12 | convolution fusion | flops 9826467840 | bytes 38454272 | tf_op jit(solution)/shard_map/rd,fd->rf/dot_general | solution.py:594
  682.1 19.2 %multiply_reduce_fusion = (f32[1088]{0:T(1024)}, f32[1024]{0:T(1024)S(1)}, f32[1024]{0:T(1024)S(1)}, f32[1088]{0:T(1024)}, f32[1024,1088]{0,1:T(8,128)S(1)}) fusion(f32[1024,1088]{0,1:T(8,128)} %copy-done.39, f32[1024]{0:T(1024)S(1)} %add_rsqrt_fusion, f32[1024]{0:T(1024)S(1)} %broadcast_multiply_fusion.8, f32[1088]{0:T(1024)S(1)} %mul.354, ...), kind=kOutput, calls=%fused_computation.68 | convolution fusion | flops 9707253760 | bytes 27325184 | tf_op jit(solution)/shard_map/rf,df->rd/dot_general | solution.py:599
  737.7 49.4 %shard_map.294 = bf16[1,4096,384]{2,1,0:T(8,128)(2,1)S(1)} custom-call(s32[1,8]{1,0:T(1,128)S(1)} %bitcast.279, s32[1]{0:T(128)S(6)} %select_n.21.nb_ref, bf16[1,4096,384]{2,1,0:T(8,128)(2,1)} %bitcast.268, bf16[1,4096,128]{2,1,0:T(8,128)(2,1)S(1)} %copy-done.7, bf16[1,4096,128]{2,1,0:T(8,128)(2,1)S(1)} %bitcast.274, f32[1,8,4096]{2,1,0:T(8,128)S(1)} %copy-done.38), custom_call_target="tpu_custom_call" | custom-call | flops 21474836480 | bytes 9830400 | tf_op jit(solution)/shard_map/pallas_call | solution.py:166
  794.5 51.7 %shard_map.293 = bf16[1,4096,384]{2,1,0:T(8,128)(2,1)} custom-call(s32[1,8]{1,0:T(1,128)S(1)} %copy-done.30, s32[1]{0:T(128)} %slice.926.nb_ref, bf16[1,4096,512]{2,1,0:T(8,128)(2,1)} %bitcast.25.x_ref, bf16[1,4096,128]{2,1,0:T(8,128)(2,1)S(1)} %copy-done.28, bf16[1,4096,256]{2,1,0:T(8,128)(2,1)S(1)} %bitcast.264, f32[1,8,4096]{2,1,0:T(8,128)S(1)} %copy-done.34), custom_call_target="tpu_custom_call" | custom-call | flops 21474836480 | bytes 9830400 | tf_op jit(solution)/shard_map/pallas_call | solution.py:166
  866.4 29.5 %all-to-all-done.11.refs_1_ = bf16[4,1024,384]{2,1,0:T(8,128)(2,1)} async-done(((bf16[4,1024,384]{2,1,0:T(8,128)(2,1)}), bf16[4,1024,384]{2,1,0:T(8,128)(2,1)}, u32[]{:S(2)}, u32[]{:S(2)}) %all-to-all-start.11) | async-done | bytes 3145760 | tf_op jit(solution)/shard_map/all_to_all | solution.py:493
  965.3 28.1 %multiply_convert_fusion = bf16[1024,4352]{1,0:T(8,128)(2,1)} fusion(bf16[1024,1088]{0,1:T(8,128)(2,1)S(1)} %copy-done.52, bf16[1,4352,1088]{2,1,0:T(8,128)(2,1)} %all-gather.23.cloned.1.call-done, f32[1024,4352]{1,0:T(8,128)} %get-tuple-element.386, f32[4352]{0:T(1024)S(1)} %copy-done.93), kind=kOutput, calls=%fused_computation.10 | convolution fusion | flops 9826467840 | bytes 38454272 | tf_op jit(solution)/shard_map/rd,fd->rf/dot_general | solution.py:594
  1013.8 19.2 %multiply_reduce_fusion.2 = (f32[1088]{0:T(1024)}, f32[1024]{0:T(1024)S(1)}, f32[1024]{0:T(1024)S(1)}, f32[1088]{0:T(1024)}, f32[1024,1088]{0,1:T(8,128)S(1)}) fusion(f32[1024,1088]{0,1:T(8,128)} %copy-done.50, f32[1024]{0:T(1024)S(1)} %copy-done.99, f32[1024]{0:T(1024)S(1)} %copy-done.75, f32[1088]{0:T(1024)S(1)} %copy-done.81, ...), kind=kOutput, calls=%fused_computation.70 | convolution fusion | flops 9707253760 | bytes 27325184 | tf_op jit(solution)/shard_map/rf,df->rd/dot_general | solution.py:599
  1085.1 50.0 %shard_map.298 = bf16[1,4096,384]{2,1,0:T(8,128)(2,1)S(1)} custom-call(s32[1,8]{1,0:T(1,128)S(1)} %bitcast.280, s32[1]{0:T(128)S(6)} %select_n.21.nb_ref, bf16[1,4096,384]{2,1,0:T(8,128)(2,1)} %bitcast.266, bf16[1,4096,128]{2,1,0:T(8,128)(2,1)S(1)} %copy-done.5, bf16[1,4096,128]{2,1,0:T(8,128)(2,1)S(1)} %bitcast.273, f32[1,8,4096]{2,1,0:T(8,128)S(1)} %copy-done.36), custom_call_target="tpu_custom_call" | custom-call | flops 21474836480 | bytes 9830400 | tf_op jit(solution)/shard_map/pallas_call | solution.py:166
  1141.7 51.8 %shard_map.297 = bf16[1,4096,384]{2,1,0:T(8,128)(2,1)} custom-call(s32[1,8]{1,0:T(1,128)S(1)} %copy-done.30, s32[1]{0:T(128)} %slice.926.nb_ref, bf16[1,4096,512]{2,1,0:T(8,128)(2,1)} %bitcast.14.x_ref, bf16[1,4096,128]{2,1,0:T(8,128)(2,1)S(1)} %copy-done.26, bf16[1,4096,256]{2,1,0:T(8,128)(2,1)S(1)} %bitcast.263, f32[1,8,4096]{2,1,0:T(8,128)S(1)} %copy-done.32), custom_call_target="tpu_custom_call" | custom-call | flops 21474836480 | bytes 9830400 | tf_op jit(solution)/shard_map/pallas_call | solution.py:166
  1212.8 28.3 %all-to-all-done.15.refs_1_ = bf16[4,1024,384]{2,1,0:T(8,128)(2,1)} async-done(((bf16[4,1024,384]{2,1,0:T(8,128)(2,1)}), bf16[4,1024,384]{2,1,0:T(8,128)(2,1)}, u32[]{:S(2)}, u32[]{:S(2)}) %all-to-all-start.15) | async-done | bytes 3145760 | tf_op jit(solution)/shard_map/all_to_all | solution.py:493
  1250.1 36.6 %reduce-scatter.15.cloned.1.call-done = bf16[136,4352]{1,0:T(8,128)(2,1)} async-done(((bf16[1088,4352]{1,0:T(8,128)(2,1)}), bf16[136,4352]{1,0:T(8,128)(2,1)}) %reduce-scatter.15.cloned.1.call-update) | async-done | bytes 1183760 | tf_op jit(solution)/shard_map/reduce_scatter | solution.py:543
  1313.8 18.0 %fusion.55 = bf16[1,1024,1088]{1,2,0:T(8,128)(2,1)} fusion(f32[1024,1088]{0,1:T(8,128)} %copy-done.39, bf16[1024,4352]{1,0:T(8,128)(2,1)} %get-tuple-element.391, bf16[1,4352,1088]{2,1,0:T(8,128)(2,1)} %all-gather.29.cloned.1.call-done, f32[1024]{0:T(1024)S(1)} %bitcast.299, f32[1088]{0:T(1024)S(1)} %add.318), kind=kOutput, calls=%fused_computation.93 | convolution fusion | flops 9701687296 | bytes 25075968 | tf_op jit(solution)/shard_map/dot_general | solution.py:539
  1414.1 54.0 %reduce-scatter.17.cloned.1.call-done = bf16[136,4352]{1,0:T(8,128)(2,1)} async-done(((bf16[1088,4352]{1,0:T(8,128)(2,1)}), bf16[136,4352]{1,0:T(8,128)(2,1)}) %reduce-scatter.17.cloned.1.call-update) | async-done | bytes 1183760 | tf_op jit(solution)/shard_map/reduce_scatter | solution.py:543
  (577 shorter events, 705.0 us)
Async XLA Ops:
  7.2 82.4 %all-gather.15.cloned.1.call-start = ((), (), s32[]{:S(2)}) async-start(), calls=%async_computation.27 | async-start | bytes 8146944 | tf_op jit(solution)/shard_map/all_gather | solution.py:478
  13.8 258.8 %all-gather.19.cloned.1.call-start = ((), (), s32[]{:S(2)}) async-start(), calls=%async_computation.35 | async-start | bytes 2820096 | tf_op jit(solution)/shard_map/all_gather | solution.py:478
  14.8 267.1 %all-gather.21.cloned.1.call-start = ((), (), s32[]{:S(2)}) async-start(), calls=%async_computation.36 | async-start | bytes 10653696 | tf_op jit(solution)/shard_map/all_gather | solution.py:478
  19.1 298.3 %all-gather.23.cloned.1.call-start = ((), (), s32[]{:S(2)}) async-start(), calls=%async_computation.37 | async-start | bytes 11280384 | tf_op jit(solution)/shard_map/all_gather | solution.py:478
  23.5 360.9 %all-gather.17.cloned.1.call-start = ((), (), s32[]{:S(2)}) async-start(), calls=%async_computation.28 | async-start | bytes 8146944 | tf_op jit(solution)/shard_map/all_gather | solution.py:478
  116.7 451.6 %all-gather.25.cloned.1.call-start = ((), (), s32[]{:S(2)}) async-start(), calls=%async_computation.38 | async-start | bytes 2820096 | tf_op jit(solution)/shard_map/all_gather | solution.py:478
  153.5 52.2 %all-to-all-start.1 = ((bf16[4,1024,512]{2,1,0:T(8,128)(2,1)}), bf16[4,1024,512]{2,1,0:T(8,128)(2,1)}, u32[]{:S(2)}, u32[]{:S(2)}) async-start(bf16[4,1024,512]{2,1,0:T(8,128)(2,1)} %pad_maximum_fusion.2), calls=%async_computation.1 | async-start | bytes 8388608 | tf_op jit(solution)/shard_map/all_to_all | solution.py:493
  158.3 419.9 %all-gather.27.cloned.1.call-start = ((), (), s32[]{:S(2)}) async-start(), calls=%async_computation.39 | async-start | bytes 10653696 | tf_op jit(solution)/shard_map/all_gather | solution.py:478
  411.9 219.4 %all-gather.29.cloned.1.call-start = ((), (), s32[]{:S(2)}) async-start(), calls=%async_computation.40 | async-start | bytes 11280384 | tf_op jit(solution)/shard_map/all_gather | solution.py:478
  448.8 52.4 %all-to-all-start.5 = ((bf16[4,1024,512]{2,1,0:T(8,128)(2,1)}), bf16[4,1024,512]{2,1,0:T(8,128)(2,1)}, u32[]{:S(2)}, u32[]{:S(2)}) async-start(bf16[4,1024,512]{2,1,0:T(8,128)(2,1)} %pad_maximum_fusion.3), calls=%async_computation.5 | async-start | bytes 8388608 | tf_op jit(solution)/shard_map/all_to_all | solution.py:493
  546.5 299.7 %reduce-scatter.7.cloned.1.call-start = ((), (), s32[]{:S(2)}) async-start(), calls=%async_computation.29 | async-start | bytes 11280384 | tf_op jit(solution)/shard_map/reduce_scatter | solution.py:543
  631.3 273.4 %reduce-scatter.9.cloned.1.call-start = ((), (), s32[]{:S(2)}) async-start(), calls=%async_computation.30 | async-start | bytes 10653696 | tf_op jit(solution)/shard_map/reduce_scatter | solution.py:543
  731.9 56.9 %all-to-all-start.9 = ((bf16[4,1024,256]{2,1,0:T(8,128)(2,1)}), bf16[4,1024,256]{2,1,0:T(8,128)(2,1)S(1)}, u32[]{:S(2)}, u32[]{:S(2)}) async-start(bf16[4,1024,256]{2,1,0:T(8,128)(2,1)} %pad_maximum_fusion.5), calls=%async_computation.9 | async-start | bytes 4194304 | tf_op jit(solution)/shard_map/all_to_all | solution.py:493
  788.8 57.4 %all-to-all-start.10 = ((bf16[4,1024,384]{2,1,0:T(8,128)(2,1)}), bf16[4,1024,384]{2,1,0:T(8,128)(2,1)}, u32[]{:S(2)}, u32[]{:S(2)}) async-start(bf16[4,1024,384]{2,1,0:T(8,128)(2,1)} %bitcast.270), calls=%async_computation.10 | async-start | bytes 6291456 | tf_op jit(solution)/shard_map/all_to_all | solution.py:493
  853.3 42.5 %all-to-all-start.11 = ((bf16[4,1024,384]{2,1,0:T(8,128)(2,1)}), bf16[4,1024,384]{2,1,0:T(8,128)(2,1)}, u32[]{:S(2)}, u32[]{:S(2)}) async-start(bf16[4,1024,384]{2,1,0:T(8,128)(2,1)} %collective-permute-done.6), calls=%async_computation.12 | async-start | bytes 6291456 | tf_op jit(solution)/shard_map/all_to_all | solution.py:493
  858.0 181.0 %all-reduce.7.cloned.1.call-start = ((), (), s32[]{:S(2)}) async-start(), calls=%async_computation.42 | async-start | bytes 4874240 | tf_op jit(solution)/shard_map/psum | solution.py:639
  904.7 175.5 %reduce-scatter.11.cloned.1.call-start = ((), (), s32[]{:S(2)}) async-start(), calls=%async_computation.31 | async-start | bytes 10653696 | tf_op jit(solution)/shard_map/reduce_scatter | solution.py:543
  924.0 269.5 %reduce-scatter.13.cloned.1.call-start = ((), (), s32[]{:S(2)}) async-start(), calls=%async_computation.32 | async-start | bytes 11280384 | tf_op jit(solution)/shard_map/reduce_scatter | solution.py:543
  963.5 323.2 %reduce-scatter.15.cloned.1.call-start = ((), (), s32[]{:S(2)}) async-start(), calls=%async_computation.33 | async-start | bytes 10653696 | tf_op jit(solution)/shard_map/reduce_scatter | solution.py:543
  1080.3 56.6 %all-to-all-start.13 = ((bf16[4,1024,256]{2,1,0:T(8,128)(2,1)}), bf16[4,1024,256]{2,1,0:T(8,128)(2,1)S(1)}, u32[]{:S(2)}, u32[]{:S(2)}) async-start(bf16[4,1024,256]{2,1,0:T(8,128)(2,1)} %pad_maximum_fusion.6), calls=%async_computation.16 | async-start | bytes 4194304 | tf_op jit(solution)/shard_map/all_to_all | solution.py:493
  1136.9 56.7 %all-to-all-start.14 = ((bf16[4,1024,384]{2,1,0:T(8,128)(2,1)}), bf16[4,1024,384]{2,1,0:T(8,128)(2,1)}, u32[]{:S(2)}, u32[]{:S(2)}) async-start(bf16[4,1024,384]{2,1,0:T(8,128)(2,1)} %bitcast.269), calls=%async_computation.17 | async-start | bytes 6291456 | tf_op jit(solution)/shard_map/all_to_all | solution.py:493
  1204.2 159.7 %all-reduce.5.cloned.1.call-start = ((), (), s32[]{:S(2)}) async-start(), calls=%async_computation.41 | async-start | bytes 4874240 | tf_op jit(solution)/shard_map/psum | solution.py:633
  1211.3 256.8 %reduce-scatter.17.cloned.1.call-start = ((), (), s32[]{:S(2)}) async-start(), calls=%async_computation.34 | async-start | bytes 10653696 | tf_op jit(solution)/shard_map/reduce_scatter | solution.py:543
  1403.3 69.2 %all-to-all-start.19 = ((bf16[4,136,1088]{2,1,0:T(8,128)(2,1)}), bf16[4,136,1088]{2,1,0:T(8,128)(2,1)}, u32[]{:S(2)}, u32[]{:S(2)}) async-start(bf16[4,136,1088]{2,1,0:T(8,128)(2,1)} %bitcast.287), calls=%async_computation.25 | async-start | bytes 2506752 | tf_op jit(solution)/shard_map/all_to_all | solution.py:493
  (146 other events, 3900.0 us)
Sparse Core Ops, SparseCore 0:
  13.9 75.6 all-gather.14
  91.3 31.5 all-gather.18
  125.0 90.0 all-gather.20
  217.2 94.0 all-gather.22
  313.4 70.9 all-gather.16
  385.9 31.4 all-gather.24
  419.1 90.0 all-gather.26
  511.4 94.0 all-gather.28
  631.4 114.1 reduce-scatter.6
  747.8 98.4 reduce-scatter.8
  904.8 72.8 all-reduce.6
  979.9 100.2 reduce-scatter.10
  1082.6 103.4 reduce-scatter.12
  1188.3 98.3 reduce-scatter.14
  1289.8 74.0 all-reduce.4
  1366.0 102.0 reduce-scatter.16
where the time goes:
time: 1580 us; the launch traced here: 1560 us
  matrix products  426 us (27%)
  Pallas kernels  426 us (27%)
  waiting for transfers between devices  382 us (24%)
  local copies, waits for them, and re-layouts  94.4 us (6%)
  other arithmetic  92.2 us (6%)
  starting transfers between devices  91.9 us (6%)
  blocking collectives  32.4 us (2%)
  between operations  16.9 us (1%)
    pallas_call x4, Pallas kernels, flash_bwd(): pl.pallas_call(functools.partial(bwd_kernel, B=B, NB=NB), out_shape=jax.S...  203 us
    all_to_all x20, waiting for transfers between devices, exchange(): return plain(lax.all_to_all(plain(x), 'ctx', 0, 0))  156 us
    pallas_call x4, Pallas kernels, flash_fwd(): pl.pallas_call(functools.partial(fwd_kernel, B=B, NB=NB), out_shape=(jax....  134 us
    reduce_scatter x6, waiting for transfers between devices, reduce_fsdp(): return lax.psum_scatter(g.astype(bf16), FS, scatter_dimension=0, tiled=True)  103 us
    all_gather x8, waiting for transfers between devices, fetch(): return lax.all_gather(w.astype(bf16), FS, axis=0, tiled=True)  87.4 us
    all_to_all x20, starting transfers between devices, exchange(): return plain(lax.all_to_all(plain(x), 'ctx', 0, 0))  83.1 us
    dot_general x2, matrix products, local(): u = jnp.dot(n2, up_w, preferred_element_type=f32) + vector(8, layer)  70.8 us
    dot_general x2, matrix products, local(): jnp.einsum('rd,fd->rf', gb, down_w, preferred_element_type=f32)  59.3 us
  transfers between devices with their start and end apart: 46, of which 21 were waited for; matrix products, arithmetic and copies ran while one was open for 36% of the time, Pallas kernels for 27%

commit v1 on v0

--- a/solution.py
+++ b/solution.py
@@ -337,6 +337,73 @@
     )(x)
 
 
+def gather_kernel(x_ref, o_ref, own_sem, zs, zr, xs, xr, cs, cr, *, Z, C, quarter):
+    z, a, c = lax.axis_index("zz"), lax.axis_index("core"), lax.axis_index("ctx")
+    mesh_id = pl.DeviceIdType.MESH
+    other = 1 - a
+    peers = [(lax.rem(z + k, Z), a, c) for k in range(1, Z)] + [(z, a, lax.rem(c + j, C)) for j in range(1, C)] + [(z, other, c)]
+    barrier = pltpu.get_barrier_semaphore()
+    for peer in peers:
+        pl.semaphore_signal(barrier, inc=1, device_id=peer, device_id_type=mesh_id)
+    pl.semaphore_wait(barrier, len(peers))
+
+    f = 2 * z + a
+
+    def cols(q):
+        return pl.ds(pl.multiple_of(q * quarter, quarter), quarter)
+
+    def send(src, dst, s, r, peer):
+        copy = pltpu.make_async_remote_copy(src_ref=src, dst_ref=dst, send_sem=s, recv_sem=r, device_id=peer, device_id_type=mesh_id)
+        copy.start()
+        return copy
+
+    along = []
+    for k in range(1, Z):
+        along.append(send(x_ref.at[:, cols(c)], o_ref.at[f, :, cols(c)], zs.at[k - 1], zr.at[k - 1], peers[k - 1]))
+    own = pltpu.make_async_copy(x_ref, o_ref.at[f], own_sem)
+    own.start()
+    whole = send(x_ref, o_ref.at[f], cs.at[0], cr.at[0], peers[-1])
+    plane, cross = [], []
+    for k in range(1, Z):
+        along[k - 1].wait_recv()
+        fs = 2 * lax.rem(z + Z - k, Z) + a
+        piece = o_ref.at[fs, :, cols(c)]
+        for j in range(1, C):
+            n = (k - 1) * (C - 1) + j - 1
+            plane.append(send(piece, piece, xs.at[n], xr.at[n], peers[Z - 1 + j - 1]))
+        n = 1 + (k - 1) * C
+        cross.append(send(piece, piece, cs.at[n], cr.at[n], peers[-1]))
+    for k in range(1, Z):
+        fs = 2 * lax.rem(z + Z - k, Z) + a
+        for j in range(1, C):
+            plane[(k - 1) * (C - 1) + j - 1].wait_recv()
+            piece = o_ref.at[fs, :, cols(lax.rem(c + C - j, C))]
+            n = 1 + (k - 1) * C + j
+            cross.append(send(piece, piece, cs.at[n], cr.at[n], peers[-1]))
+    for copy in along + plane:
+        copy.wait_send()
+    whole.wait_send()
+    whole.wait_recv()
+    for copy in cross:
+        copy.wait_send()
+        copy.wait_recv()
+    own.wait()
+
+
+def gather_all(x, Z, C):
+    R, W = x.shape
+    dma = pltpu.SemaphoreType.DMA
+    n, m = (Z - 1) * (C - 1), 1 + (Z - 1) * C
+    return pl.pallas_call(functools.partial(gather_kernel, Z=Z, C=C, quarter=W // C),
+        out_shape=jax.ShapeDtypeStruct((2 * Z, R, W), bf16),
+        in_specs=[pl.BlockSpec(memory_space=pl.ANY)],
+        out_specs=pl.BlockSpec(memory_space=pl.ANY),
+        scratch_shapes=[dma(()), dma((Z - 1,)), dma((Z - 1,)), dma((n,)), dma((n,)), dma((m,)), dma((m,))],
+        compiler_params=pltpu.CompilerParams(collective_id=0, has_side_effects=True, vmem_limit_bytes=56 << 20),
+        cost_estimate=pl.CostEstimate(flops=0, bytes_accessed=20 * R * W * Z, transcendentals=0),
+    )(x)
+
+
 def join_kernel(*refs, count):
     t = pl.program_id(0)
     stacks, tail, out = refs[:-2], refs[-2], refs[-1]
@@ -380,6 +447,73 @@
         out_specs=pl.BlockSpec((1, R, W), lambda t: (t, 0, 0)),
         compiler_params=pltpu.CompilerParams(vmem_limit_bytes=56 << 20),
         cost_estimate=pl.CostEstimate(flops=0, bytes_accessed=4 * R * C * W, transcendentals=0),
+    )(x)
+
+
+def gather_kernel(x_ref, o_ref, own_sem, zs, zr, xs, xr, cs, cr, *, Z, C, quarter):
+    z, a, c = lax.axis_index("zz"), lax.axis_index("core"), lax.axis_index("ctx")
+    mesh_id = pl.DeviceIdType.MESH
+    other = 1 - a
+    peers = [(lax.rem(z + k, Z), a, c) for k in range(1, Z)] + [(z, a, lax.rem(c + j, C)) for j in range(1, C)] + [(z, other, c)]
+    barrier = pltpu.get_barrier_semaphore()
+    for peer in peers:
+        pl.semaphore_signal(barrier, inc=1, device_id=peer, device_id_type=mesh_id)
+    pl.semaphore_wait(barrier, len(peers))
+
+    f = 2 * z + a
+
+    def cols(q):
+        return pl.ds(pl.multiple_of(q * quarter, quarter), quarter)
+
+    def send(src, dst, s, r, peer):
+        copy = pltpu.make_async_remote_copy(src_ref=src, dst_ref=dst, send_sem=s, recv_sem=r, device_id=peer, device_id_type=mesh_id)
+        copy.start()
+        return copy
+
+    along = []
+    for k in range(1, Z):
+        along.append(send(x_ref.at[:, cols(c)], o_ref.at[f, :, cols(c)], zs.at[k - 1], zr.at[k - 1], peers[k - 1]))
+    own = pltpu.make_async_copy(x_ref, o_ref.at[f], own_sem)
+    own.start()
+    whole = send(x_ref, o_ref.at[f], cs.at[0], cr.at[0], peers[-1])
+    plane, cross = [], []
+    for k in range(1, Z):
+        along[k - 1].wait_recv()
+        fs = 2 * lax.rem(z + Z - k, Z) + a
+        piece = o_ref.at[fs, :, cols(c)]
+        for j in range(1, C):
+            n = (k - 1) * (C - 1) + j - 1
+            plane.append(send(piece, piece, xs.at[n], xr.at[n], peers[Z - 1 + j - 1]))
+        n = 1 + (k - 1) * C
+        cross.append(send(piece, piece, cs.at[n], cr.at[n], peers[-1]))
+    for k in range(1, Z):
+        fs = 2 * lax.rem(z + Z - k, Z) + a
+        for j in range(1, C):
+            plane[(k - 1) * (C - 1) + j - 1].wait_recv()
+            piece = o_ref.at[fs, :, cols(lax.rem(c + C - j, C))]
+            n = 1 + (k - 1) * C + j
+            cross.append(send(piece, piece, cs.at[n], cr.at[n], peers[-1]))
+    for copy in along + plane:
+        copy.wait_send()
+    whole.wait_send()
+    whole.wait_recv()
+    for copy in cross:
+        copy.wait_send()
+        copy.wait_recv()
+    own.wait()
+
+
+def gather_all(x, Z, C):
+    R, W = x.shape
+    dma = pltpu.SemaphoreType.DMA
+    n, m = (Z - 1) * (C - 1), 1 + (Z - 1) * C
+    return pl.pallas_call(functools.partial(gather_kernel, Z=Z, C=C, quarter=W // C),
+        out_shape=jax.ShapeDtypeStruct((2 * Z, R, W), bf16),
+        in_specs=[pl.BlockSpec(memory_space=pl.ANY)],
+        out_specs=pl.BlockSpec(memory_space=pl.ANY),
+        scratch_shapes=[dma(()), dma((Z - 1,)), dma((Z - 1,)), dma((n,)), dma((n,)), dma((m,)), dma((m,))],
+        compiler_params=pltpu.CompilerParams(collective_id=0, has_side_effects=True, vmem_limit_bytes=56 << 20),
+        cost_estimate=pl.CostEstimate(flops=0, bytes_accessed=20 * R * W * Z, transcendentals=0),
     )(x)
 
 
@@ -449,15 +583,6 @@
     own_pos = (lax.dynamic_slice_in_dim(order, 2 * me, 2, 0)[:, None] * B + jnp.arange(B, dtype=jnp.int32)).reshape(rows, 1)
     live = (own_pos < lengths[0]).astype(f32)
 
-    vectors = [ln1_gain, ln1_bias, q_bias, v_bias, out_bias, ln2_gain, ln2_bias, down_bias, up_bias]
-    vec = jnp.concatenate(vectors, axis=1).astype(bf16)
-    vec = lax.all_gather(vec, FS).astype(f32)
-
-    def vector(index, layer):
-        if index < 8:
-            return vec[:, layer, index * shard:(index + 1) * shard].reshape(-1)
-        return vec[:, layer, 8 * shard:].reshape(-1)
-
     def pack(w):
         parts = []
         for g in range(G):
@@ -477,10 +602,29 @@
     def fetch(w):
         return lax.all_gather(w.astype(bf16), FS, axis=0, tiled=True)
 
+    vectors = [ln1_gain, ln1_bias, q_bias, v_bias, out_bias, ln2_gain, ln2_bias, down_bias]
+    vec = [t.astype(bf16).T for t in vectors] + [up_bias.astype(bf16).reshape(4 * L, shard).T]
+    first = pack(qkv_weight[0].astype(bf16))
+    block = jnp.concatenate([first] + vec, axis=1)
+    used = block.shape[1]
+    if C == 4 and lax.axis_size("zz") == 4:
+        block = jnp.pad(block, ((0, 0), (0, -used % (128 * C))))
+        block = gather_all(block, 4, C)
+    else:
+        block = lax.all_gather(block, FS)
+    first_w = block[:, :, :3 * width].reshape(width, 3 * width)
+    vec = jnp.transpose(block[:, :, 3 * width:used].reshape(width, used - 3 * width)).astype(f32)
+
+    def vector(index, layer):
+        if index < 8:
+            return vec[L * index + layer]
+        t = vec[8 * L + 4 * layer:8 * L + 4 * layer + 4]
+        return jnp.transpose(t.reshape(4, -1, shard), (1, 0, 2)).reshape(-1)
+
     weights = []
     for layer in range(L):
         weights.append((
-            fetch(pack(qkv_weight[layer].astype(bf16))),
+            fetch(pack(qkv_weight[layer].astype(bf16))) if layer else first_w,
             fetch(out_weight[layer]),
             fetch(up_weight[layer]),
             fetch(down_weight[layer]),
@@ -628,32 +772,37 @@
             t = flash_bwd(heads[s], o[s], d_oh[s], lse[s], phase_inv[s], phase_nb[s], B)
             t = t.reshape(C, rows, 384)
             if s:
-                t, d_wide[0], d_down = after(t, d_wide[0], d_down)
-            if s == S - 1 and layer < L - 1:
-                four_sum = lax.psum((fours[layer + 1], d_down), "ctx")
+                t, d_wide[0] = after(t, d_wide[0])
+            if s == S - 1:
+                t, d_down = after(t, d_down)
+            if s == S - 1 and layer:
+                t, d_up = after(t, d_up)
+                ffn_sum = lax.psum((d_up, d_down), "ctx")
             d_wide.append(exchange(swap(t) if s else t))
         d_tail = jnp.concatenate([dkv16.astype(bf16), dq16], axis=1)
         d_row = join(d_wide, d_tail)
-        d_row, d_up = after(d_row, d_up)
-        if layer:
-            ffn_sum = lax.psum((d_up, d_down), "ctx")
-        else:
-            up_sum = ctx_sum([d_up])
+        d_back = d_row
+        if layer == 0:
+            d_row, d_up = after(d_row, d_up)
+            mine, middle_sizes = ctx_begin([fours[1], d_up, d_down])
+            d_back, mine = after(d_row, mine)
+            middle = ctx_end(mine)
         d_qkv = jnp.einsum("rd,rc->dc", n1, d_row, preferred_element_type=f32).astype(bf16)
         d_four = jnp.concatenate([d_qkv, d_out], axis=1)
         if layer:
             d_row, d_four = after(d_row, plain(d_four))
         d_four = reduce_fsdp(d_four)
         sums = unpack(col_sum(d_row)[None])[0]
-        dn1 = jnp.einsum("rc,dc->rd", d_row, qkv_w, preferred_element_type=f32)
+        dn1 = jnp.einsum("rc,dc->rd", d_back, qkv_w, preferred_element_type=f32)
         back, d_gain1, d_bias1 = norm_back(dn1, stream_in, vector(0, layer))
         grad = gm + back
         fours[layer] = d_four
         ffns[layer] = (d_up, d_down)
         if layer == 0:
             last = ctx_sum([d_four])
-            matrices[1] = [four_sum[0].astype(f32), ffn_sum[0].astype(f32), ffn_sum[1].astype(f32)]
-            matrices[0] = spread(last, [wide_shape]) + spread(up_sum, [wide_shape]) + [four_sum[1].astype(f32)]
+            rest = spread((middle, middle_sizes), [wide_shape, wide_shape, tall_shape])
+            matrices[1] = [rest[0], ffn_sum[0].astype(f32), ffn_sum[1].astype(f32)]
+            matrices[0] = spread(last, [wide_shape]) + rest[1:]
         small[layer] = jnp.concatenate([
             t.reshape(-1, n) for t, n in (
                 (d_gain1, shard), (d_bias1, shard), (sums[:width], shard), (sums[2 * width:], shard), (d_out_b, shard),

time: 1580 us -> 1530 us (0.968)
  Pallas kernels: 426 us -> 279 us
  waiting for transfers between devices: 382 us -> 472 us
    all_to_all x20, waiting for transfers between devices: 156 us -> 313 us  [exchange(): return plain(lax.all_to_all(plain(x), 'ctx', 0, 0))]
    pallas_call x4, Pallas kernels: 203 us -> 97.5 us  [flash_bwd(): pl.pallas_call(functools.partial(bwd_kernel, B=B, NB=NB), out_shape=jax.S...]
    all_gather x8 -> x7, waiting for transfers between devices: 87.4 us -> 0.1 us  [fetch(): return lax.all_gather(w.astype(bf16), FS, axis=0, tiled=True)]
    pallas_call x4, Pallas kernels: 134 us -> 63 us  [flash_fwd(): pl.pallas_call(functools.partial(fwd_kernel, B=B, NB=NB), out_shape=(jax....]
    pallas_call x0 -> x1, Pallas kernels: none -> 54.5 us  [gather_all(): pl.pallas_call(functools.partial(gather_kernel, Z=Z, C=C, quarter=W // C)...]
    reduce_scatter x6, waiting for transfers between devices: 103 us -> 141 us  [reduce_fsdp(): return lax.psum_scatter(g.astype(bf16), FS, scatter_dimension=0, tiled=True)]
    psum x1 -> x0, waiting for transfers between devices: 16.2 us -> none  [local(): four_sum = lax.psum((fours[layer + 1], d_down), 'ctx')]
    all_gather x1 -> x0, blocking collectives: 15.9 us -> none  [local(): vec = lax.all_gather(vec, FS).astype(f32)]
  transfers between devices with their start and end apart: 46 -> 43, of which waited for: 21 -> 23; matrix products, arithmetic and copies ran while one was open for 36% -> 36% of each run, Pallas kernels for 27% -> 18%
where the time goes in v1:
time: 1530 us; the launch traced here: 1510 us
  waiting for transfers between devices  472 us (31%)
  matrix products  421 us (28%)
  Pallas kernels  279 us (18%)
  local copies, waits for them, and re-layouts  103 us (7%)
  other arithmetic  96.3 us (6%)
  starting transfers between devices  88.2 us (6%)
  blocking collectives  38.2 us (2%)
  between operations  17.2 us (1%)
    all_to_all x20, waiting for transfers between devices, exchange(): return plain(lax.all_to_all(plain(x), 'ctx', 0, 0))  313 us
    reduce_scatter x6, waiting for transfers between devices, reduce_fsdp(): return lax.psum_scatter(g.astype(bf16), FS, scatter_dimension=0, tiled=True)  141 us
    pallas_call x4, Pallas kernels, flash_bwd(): pl.pallas_call(functools.partial(bwd_kernel, B=B, NB=NB), out_shape=jax.S...  97.5 us
    all_to_all x20, starting transfers between devices, exchange(): return plain(lax.all_to_all(plain(x), 'ctx', 0, 0))  85.2 us
    dot_general x2, matrix products, local(): u = jnp.dot(n2, up_w, preferred_element_type=f32) + vector(8, layer)  70.5 us
    pallas_call x4, Pallas kernels, flash_fwd(): pl.pallas_call(functools.partial(fwd_kernel, B=B, NB=NB), out_shape=(jax....  63 us
    dot_general x2, matrix products, local(): jnp.einsum('rd,fd->rf', gb, down_w, preferred_element_type=f32)  59.3 us
    pallas_call x1, Pallas kernels, gather_all(): pl.pallas_call(functools.partial(gather_kernel, Z=Z, C=C, quarter=W // C)...  54.5 us
  transfers between devices with their start and end apart: 43, of which 23 were waited for; matrix products, arithmetic and copies ran while one was open for 36% of the time, Pallas kernels for 18%

profile of v1, /device:TPU:0, one launch (start us, length us, event | category | flops | bytes accessed | tf_op | source)
XLA Modules:
  0.0 1514.6 jit_solution(13377027238989304711)
XLA Ops:
  30.9 54.5 %shard_map.280 = bf16[8,136,3584]{2,1,0:T(8,128)(2,1)} custom-call(bf16[136,3584]{1,0:T(8,128)(2,1)} %pad.4.x_ref), custom_call_target="tpu_custom_call" | custom-call | bytes 38993920 | tf_op jit(solution)/shard_map/pallas_call | solution.py:510
  128.2 31.5 %all-to-all-done = bf16[4,1024,384]{2,1,0:T(8,128)(2,1)S(1)} async-done(((bf16[4,1024,384]{2,1,0:T(8,128)(2,1)}), bf16[4,1024,384]{2,1,0:T(8,128)(2,1)S(1)}, u32[]{:S(2)}, u32[]{:S(2)}) %all-to-all-start) | async-done | bytes 3145760 | tf_op jit(solution)/shard_map/all_to_all | solution.py:637
  173.4 38.6 %all-to-all-done.1 = bf16[4,1024,512]{2,1,0:T(8,128)(2,1)} async-done(((bf16[4,1024,512]{2,1,0:T(8,128)(2,1)}), bf16[4,1024,512]{2,1,0:T(8,128)(2,1)}, u32[]{:S(2)}, u32[]{:S(2)}) %all-to-all-start.1) | async-done | bytes 4194336 | tf_op jit(solution)/shard_map/all_to_all | solution.py:637
  215.6 26.9 %shard_map.283 = (bf16[1,4096,128]{2,1,0:T(8,128)(2,1)S(1)}, f32[1,8,4096]{2,1,0:T(8,128)S(1)}) custom-call(s32[1,8]{1,0:T(1,128)S(1)} %slice_bitcast_fusion.9.inv_ref, s32[1]{0:T(128)} %slice.941.nb_ref, bf16[1,4096,512]{2,1,0:T(8,128)(2,1)} %bitcast.18.x_ref), custom_call_target="tpu_custom_call" | custom-call | flops 8589934592 | bytes 4194304 | tf_op jit(solution)/shard_map/pallas_call | solution.py:88
  279.7 35.2 %multiply_convert_fusion.3 = (bf16[1024,4352]{1,0:T(8,128)(2,1)}, f32[1024,4352]{1,0:T(8,128)}) fusion(f32[4352]{0:T(1024)S(1)} %add.285, bf16[1,1088,4352]{2,1,0:T(8,128)(2,1)} %all-gather.18.cloned.1.call-done, f32[1024,1088]{0,1:T(8,128)} %copy-done.51, f32[1088]{0:T(1024)S(1)} %copy-done.95, f32[1088]{0:T(1024)S(1)} %get-tuple-element.155, ...), kind=kOutput, calls=%fused_computation.15 | convolution fusion | flops 9809756160 | bytes 40699392 | tf_op jit(solution)/shard_map/dot_general | solution.py:678
  315.0 17.7 %fusion.156 = (f32[1024]{0:T(1024)S(1)}, f32[1024,1088]{0,1:T(8,128)}) fusion(f32[1088]{0:T(1024)S(1)} %copy-done.101, f32[1024,1088]{0,1:T(8,128)} %copy-done.51, bf16[1024,4352]{1,0:T(8,128)(2,1)} %get-tuple-element.394, bf16[1,4352,1088]{2,1,0:T(8,128)(2,1)} %all-gather.20.cloned.1.call-done), kind=kOutput, calls=%fused_computation.285 | convolution fusion | flops 9700572160 | bytes 27304192 | tf_op jit(solution)/shard_map/dot_general | solution.py:683
  369.4 30.7 %all-to-all-done.4 = bf16[4,1024,384]{2,1,0:T(8,128)(2,1)S(1)} async-done(((bf16[4,1024,384]{2,1,0:T(8,128)(2,1)}), bf16[4,1024,384]{2,1,0:T(8,128)(2,1)S(1)}, u32[]{:S(2)}, u32[]{:S(2)}) %all-to-all-start.4) | async-done | bytes 3145760 | tf_op jit(solution)/shard_map/all_to_all | solution.py:637
  411.4 41.2 %all-to-all-done.5 = bf16[4,1024,512]{2,1,0:T(8,128)(2,1)} async-done(((bf16[4,1024,512]{2,1,0:T(8,128)(2,1)}), bf16[4,1024,512]{2,1,0:T(8,128)(2,1)}, u32[]{:S(2)}, u32[]{:S(2)}) %all-to-all-start.5) | async-done | bytes 4194336 | tf_op jit(solution)/shard_map/all_to_all | solution.py:637
  456.3 26.9 %shard_map.289 = (bf16[1,4096,128]{2,1,0:T(8,128)(2,1)S(1)}, f32[1,8,4096]{2,1,0:T(8,128)S(1)}) custom-call(s32[1,8]{1,0:T(1,128)S(1)} %slice_bitcast_fusion.9.inv_ref, s32[1]{0:T(128)} %slice.941.nb_ref, bf16[1,4096,512]{2,1,0:T(8,128)(2,1)} %bitcast.30.x_ref), custom_call_target="tpu_custom_call" | custom-call | flops 8589934592 | bytes 4194304 | tf_op jit(solution)/shard_map/pallas_call | solution.py:88
  520.9 35.3 %multiply_convert_fusion.2 = (bf16[1024,4352]{1,0:T(8,128)(2,1)}, f32[1024,4352]{1,0:T(8,128)}) fusion(f32[4352]{0:T(1024)S(1)} %add.312, bf16[1,1088,4352]{2,1,0:T(8,128)(2,1)} %all-gather.24.cloned.1.call-done, f32[1024,1088]{0,1:T(8,128)} %copy-done.39, f32[1088]{0:T(1024)S(1)} %copy-done.99, f32[1088]{0:T(1024)S(1)} %copy-done.66, ...), kind=kOutput, calls=%fused_computation.14 | convolution fusion | flops 9809756160 | bytes 40699392 | tf_op jit(solution)/shard_map/dot_general | solution.py:678
  556.2 17.7 %convolution_convert_fusion.3 = bf16[4352,1088]{1,0:T(8,128)(2,1)} fusion(bf16[1024,4352]{1,0:T(8,128)(2,1)} %get-tuple-element.400, bf16[1024,1088]{0,1:T(8,128)(2,1)S(1)} %copy-done.55), kind=kOutput, calls=%fused_computation.7 | convolution fusion | flops 9701965824 | bytes 20611072 | tf_op jit(solution)/shard_map/rf,rd->fd/dot_general | solution.py:735
  574.0 31.2 %multiply_convert_fusion.1 = bf16[1024,4352]{1,0:T(8,128)(2,1)} fusion(bf16[1024,1088]{0,1:T(8,128)(2,1)} %fusion.55, bf16[1,4352,1088]{2,1,0:T(8,128)(2,1)} %all-gather.26.cloned.1.call-done, f32[1024,4352]{1,0:T(8,128)} %get-tuple-element.401, f32[4352]{0:T(1024)S(1)} %add.312), kind=kOutput, calls=%fused_computation.12 | convolution fusion | flops 9826467840 | bytes 38454272 | tf_op jit(solution)/shard_map/rd,fd->rf/dot_general | solution.py:738
  624.2 19.2 %multiply_reduce_fusion = (f32[1088]{0:T(1024)}, f32[1024]{0:T(1024)S(1)}, f32[1024]{0:T(1024)S(1)}, f32[1088]{0:T(1024)}, f32[1024,1088]{0,1:T(8,128)S(1)}) fusion(f32[1024,1088]{0,1:T(8,128)} %copy-done.39, f32[1024]{0:T(1024)S(1)} %add_rsqrt_fusion, f32[1024]{0:T(1024)S(1)} %broadcast_multiply_fusion.8, f32[1088]{0:T(1024)S(1)} %copy-done.66, ...), kind=kOutput, calls=%fused_computation.73 | convolution fusion | flops 9707253760 | bytes 27325184 | tf_op jit(solution)/shard_map/rf,df->rd/dot_general | solution.py:743
  705.2 40.4 %shard_map.294 = bf16[1,4096,384]{2,1,0:T(8,128)(2,1)} custom-call(s32[1,8]{1,0:T(1,128)S(1)} %copy-done.30, s32[1]{0:T(128)} %slice.941.nb_ref, bf16[1,4096,512]{2,1,0:T(8,128)(2,1)} %bitcast.30.x_ref, bf16[1,4096,128]{2,1,0:T(8,128)(2,1)S(1)} %copy-done.28, bf16[1,4096,256]{2,1,0:T(8,128)(2,1)S(1)} %bitcast.274, f32[1,8,4096]{2,1,0:T(8,128)S(1)} %copy-done.34), custom_call_target="tpu_custom_call" | custom-call | flops 21474836480 | bytes 9830400 | tf_op jit(solution)/shard_map/pallas_call | solution.py:166
  745.6 73.5 %reduce-scatter.9.cloned.1.call-done = bf16[136,4352]{1,0:T(8,128)(2,1)} async-done(((bf16[1088,4352]{1,0:T(8,128)(2,1)}), bf16[136,4352]{1,0:T(8,128)(2,1)}) %reduce-scatter.9.cloned.1.call-update) | async-done | bytes 1183760 | tf_op jit(solution)/shard_map/reduce_scatter | solution.py:687
  838.5 41.3 %all-to-all-done.11.refs_1_ = bf16[4,1024,384]{2,1,0:T(8,128)(2,1)} async-done(((bf16[4,1024,384]{2,1,0:T(8,128)(2,1)}), bf16[4,1024,384]{2,1,0:T(8,128)(2,1)}, u32[]{:S(2)}, u32[]{:S(2)}) %all-to-all-start.11) | async-done | bytes 3145760 | tf_op jit(solution)/shard_map/all_to_all | solution.py:637
  948.9 28.1 %multiply_convert_fusion = bf16[1024,4352]{1,0:T(8,128)(2,1)} fusion(bf16[1024,1088]{0,1:T(8,128)(2,1)S(1)} %copy-done.53, bf16[1,4352,1088]{2,1,0:T(8,128)(2,1)} %all-gather.20.cloned.1.call-done, f32[1024,4352]{1,0:T(8,128)} %get-tuple-element.395, f32[4352]{0:T(1024)S(1)} %copy-done.85), kind=kOutput, calls=%fused_computation.10 | convolution fusion | flops 9826467840 | bytes 38454272 | tf_op jit(solution)/shard_map/rd,fd->rf/dot_general | solution.py:738
  997.3 19.5 %multiply_reduce_fusion.2 = (f32[1088]{0:T(1024)}, f32[1024]{0:T(1024)S(1)}, f32[1024]{0:T(1024)S(1)}, f32[1088]{0:T(1024)S(1)}, f32[1024,1088]{0,1:T(8,128)S(1)}) fusion(f32[1024,1088]{0,1:T(8,128)} %copy-done.51, f32[1024]{0:T(1024)S(1)} %copy-done.91, f32[1024]{0:T(1024)S(1)} %copy-done.75, f32[1088]{0:T(1024)S(1)} %copy-done.81, ...), kind=kOutput, calls=%fused_computation.75 | convolution fusion | flops 9707253760 | bytes 27325184 | tf_op jit(solution)/shard_map/rf,df->rd/dot_general | solution.py:743
  1082.7 40.3 %shard_map.298 = bf16[1,4096,384]{2,1,0:T(8,128)(2,1)} custom-call(s32[1,8]{1,0:T(1,128)S(1)} %copy-done.30, s32[1]{0:T(128)} %slice.941.nb_ref, bf16[1,4096,512]{2,1,0:T(8,128)(2,1)} %bitcast.18.x_ref, bf16[1,4096,128]{2,1,0:T(8,128)(2,1)S(1)} %copy-done.26, bf16[1,4096,256]{2,1,0:T(8,128)(2,1)S(1)} %bitcast.275, f32[1,8,4096]{2,1,0:T(8,128)S(1)} %copy-done.32), custom_call_target="tpu_custom_call" | custom-call | flops 21474836480 | bytes 9830400 | tf_op jit(solution)/shard_map/pallas_call | solution.py:166
  1123.0 23.2 %reduce-scatter.13.cloned.1.call-done = bf16[544,1088]{1,0:T(8,128)(2,1)} async-done(((bf16[4352,1088]{1,0:T(8,128)(2,1)}), bf16[544,1088]{1,0:T(8,128)(2,1)}) %reduce-scatter.13.cloned.1.call-update) | async-done | bytes 1183760 | tf_op jit(solution)/shard_map/reduce_scatter | solution.py:687
  1165.0 28.6 %all-to-all-done.15.refs_1_ = bf16[4,1024,384]{2,1,0:T(8,128)(2,1)} async-done(((bf16[4,1024,384]{2,1,0:T(8,128)(2,1)}), bf16[4,1024,384]{2,1,0:T(8,128)(2,1)}, u32[]{:S(2)}, u32[]{:S(2)}) %all-to-all-start.15) | async-done | bytes 3145760 | tf_op jit(solution)/shard_map/all_to_all | solution.py:637
  1202.9 44.1 %reduce-scatter.15.cloned.1.call-done = bf16[136,4352]{1,0:T(8,128)(2,1)} async-done(((bf16[1088,4352]{1,0:T(8,128)(2,1)}), bf16[136,4352]{1,0:T(8,128)(2,1)}) %reduce-scatter.15.cloned.1.call-update) | async-done | bytes 1183760 | tf_op jit(solution)/shard_map/reduce_scatter | solution.py:687
  1303.5 34.7 %all-to-all-done.16 = bf16[4,408,1088]{2,1,0:T(8,128)(2,1)} async-done(((bf16[4,408,1088]{2,1,0:T(8,128)(2,1)}), bf16[4,408,1088]{2,1,0:T(8,128)(2,1)}, u32[]{:S(2)}, u32[]{:S(2)}) %all-to-all-start.16) | async-done | bytes 3551264 | tf_op jit(solution)/shard_map/all_to_all | solution.py:637
  1398.6 27.5 %psum.23 = f32[2,1632]{1,0:T(2,128)S(1)} all-reduce(f32[2,1632]{1,0:T(2,128)S(1)} %reduce_sum.342), channel_id=1, replica_groups=mesh['zz'=4,'core'=2,'ctx'=4] {'ctx'}, use_global_device_ids=true, to_apply=%region_36.37 | all-reduce | flops 3264 | bytes 26112 | tf_op jit(solution)/shard_map/psum | solution.py:813
  (580 shorter events, 689.6 us)
Async XLA Ops:
  7.2 263.8 %all-gather.16.cloned.1.call-start = ((), (), s32[]{:S(2)}) async-start(), calls=%async_computation.34 | async-start | bytes 2820096 | tf_op jit(solution)/shard_map/all_gather | solution.py:603
  9.5 270.2 %all-gather.18.cloned.1.call-start = ((), (), s32[]{:S(2)}) async-start(), calls=%async_computation.35 | async-start | bytes 10653696 | tf_op jit(solution)/shard_map/all_gather | solution.py:603
  13.7 301.3 %all-gather.20.cloned.1.call-start = ((), (), s32[]{:S(2)}) async-start(), calls=%async_computation.36 | async-start | bytes 11280384 | tf_op jit(solution)/shard_map/all_gather | solution.py:603
  18.1 317.5 %all-gather.14.cloned.1.call-start = ((), (), s32[]{:S(2)}) async-start(), calls=%async_computation.27 | async-start | bytes 8146944 | tf_op jit(solution)/shard_map/all_gather | solution.py:603
  119.2 40.5 %all-to-all-start = ((bf16[4,1024,384]{2,1,0:T(8,128)(2,1)}), bf16[4,1024,384]{2,1,0:T(8,128)(2,1)S(1)}, u32[]{:S(2)}, u32[]{:S(2)}) async-start(bf16[4,1024,384]{2,1,0:T(8,128)(2,1)} %shard_map.282), calls=%async_computation | async-start | bytes 6291456 | tf_op jit(solution)/shard_map/all_to_all | solution.py:637
  123.0 387.9 %all-gather.22.cloned.1.call-start = ((), (), s32[]{:S(2)}) async-start(), calls=%async_computation.37 | async-start | bytes 2820096 | tf_op jit(solution)/shard_map/all_gather | solution.py:603
  159.7 52.3 %all-to-all-start.1 = ((bf16[4,1024,512]{2,1,0:T(8,128)(2,1)}), bf16[4,1024,512]{2,1,0:T(8,128)(2,1)}, u32[]{:S(2)}, u32[]{:S(2)}) async-start(bf16[4,1024,512]{2,1,0:T(8,128)(2,1)} %pad_maximum_fusion.2), calls=%async_computation.1 | async-start | bytes 8388608 | tf_op jit(solution)/shard_map/all_to_all | solution.py:637
  164.6 356.2 %all-gather.24.cloned.1.call-start = ((), (), s32[]{:S(2)}) async-start(), calls=%async_computation.38 | async-start | bytes 10653696 | tf_op jit(solution)/shard_map/all_gather | solution.py:603
  359.3 40.8 %all-to-all-start.4 = ((bf16[4,1024,384]{2,1,0:T(8,128)(2,1)}), bf16[4,1024,384]{2,1,0:T(8,128)(2,1)S(1)}, u32[]{:S(2)}, u32[]{:S(2)}) async-start(bf16[4,1024,384]{2,1,0:T(8,128)(2,1)} %shard_map.288), calls=%async_computation.4 | async-start | bytes 6291456 | tf_op jit(solution)/shard_map/all_to_all | solution.py:637
  363.1 210.8 %all-gather.26.cloned.1.call-start = ((), (), s32[]{:S(2)}) async-start(), calls=%async_computation.39 | async-start | bytes 11280384 | tf_op jit(solution)/shard_map/all_gather | solution.py:603
  400.1 52.5 %all-to-all-start.5 = ((bf16[4,1024,512]{2,1,0:T(8,128)(2,1)}), bf16[4,1024,512]{2,1,0:T(8,128)(2,1)}, u32[]{:S(2)}, u32[]{:S(2)}) async-start(bf16[4,1024,512]{2,1,0:T(8,128)(2,1)} %pad_maximum_fusion.3), calls=%async_computation.5 | async-start | bytes 8388608 | tf_op jit(solution)/shard_map/all_to_all | solution.py:637
  490.3 255.3 %reduce-scatter.7.cloned.1.call-start = ((), (), s32[]{:S(2)}) async-start(), calls=%async_computation.28 | async-start | bytes 11280384 | tf_op jit(solution)/shard_map/reduce_scatter | solution.py:687
  573.9 245.3 %reduce-scatter.9.cloned.1.call-start = ((), (), s32[]{:S(2)}) async-start(), calls=%async_computation.29 | async-start | bytes 10653696 | tf_op jit(solution)/shard_map/reduce_scatter | solution.py:687
  699.7 46.0 %all-to-all-start.10 = ((bf16[4,1024,384]{2,1,0:T(8,128)(2,1)}), bf16[4,1024,384]{2,1,0:T(8,128)(2,1)}, u32[]{:S(2)}, u32[]{:S(2)}) async-start(bf16[4,1024,384]{2,1,0:T(8,128)(2,1)} %bitcast.281), calls=%async_computation.10 | async-start | bytes 6291456 | tf_op jit(solution)/shard_map/all_to_all | solution.py:637
  825.2 54.7 %all-to-all-start.11 = ((bf16[4,1024,384]{2,1,0:T(8,128)(2,1)}), bf16[4,1024,384]{2,1,0:T(8,128)(2,1)}, u32[]{:S(2)}, u32[]{:S(2)}) async-start(bf16[4,1024,384]{2,1,0:T(8,128)(2,1)} %collective-permute-done.6), calls=%async_computation.13 | async-start | bytes 6291456 | tf_op jit(solution)/shard_map/all_to_all | solution.py:637
  829.9 193.0 %all-reduce.4.cloned.1.call-start = ((), (), s32[]{:S(2)}) async-start(), calls=%async_computation.40 | async-start | bytes 4874240 | tf_op jit(solution)/shard_map/psum | solution.py:780
  838.5 210.8 %reduce-scatter.11.cloned.1.call-start = ((), (), s32[]{:S(2)}) async-start(), calls=%async_computation.30 | async-start | bytes 10653696 | tf_op jit(solution)/shard_map/reduce_scatter | solution.py:687
  907.4 238.7 %reduce-scatter.13.cloned.1.call-start = ((), (), s32[]{:S(2)}) async-start(), calls=%async_computation.31 | async-start | bytes 11280384 | tf_op jit(solution)/shard_map/reduce_scatter | solution.py:687
  947.3 299.6 %reduce-scatter.15.cloned.1.call-start = ((), (), s32[]{:S(2)}) async-start(), calls=%async_computation.32 | async-start | bytes 10653696 | tf_op jit(solution)/shard_map/reduce_scatter | solution.py:687
  1078.0 45.0 %all-to-all-start.14 = ((bf16[4,1024,384]{2,1,0:T(8,128)(2,1)}), bf16[4,1024,384]{2,1,0:T(8,128)(2,1)}, u32[]{:S(2)}, u32[]{:S(2)}) async-start(bf16[4,1024,384]{2,1,0:T(8,128)(2,1)} %bitcast.280), calls=%async_computation.17 | async-start | bytes 6291456 | tf_op jit(solution)/shard_map/all_to_all | solution.py:637
  1152.1 41.5 %all-to-all-start.15 = ((bf16[4,1024,384]{2,1,0:T(8,128)(2,1)}), bf16[4,1024,384]{2,1,0:T(8,128)(2,1)}, u32[]{:S(2)}, u32[]{:S(2)}) async-start(bf16[4,1024,384]{2,1,0:T(8,128)(2,1)} %collective-permute-done.8), calls=%async_computation.19 | async-start | bytes 6291456 | tf_op jit(solution)/shard_map/all_to_all | solution.py:637
  1156.8 286.9 %reduce-scatter.17.cloned.1.call-start = ((), (), s32[]{:S(2)}) async-start(), calls=%async_computation.33 | async-start | bytes 10653696 | tf_op jit(solution)/shard_map/reduce_scatter | solution.py:687
  1293.0 45.2 %all-to-all-start.16 = ((bf16[4,408,1088]{2,1,0:T(8,128)(2,1)}), bf16[4,408,1088]{2,1,0:T(8,128)(2,1)}, u32[]{:S(2)}, u32[]{:S(2)}) async-start(bf16[4,408,1088]{2,1,0:T(8,128)(2,1)} %pad_maximum_fusion.4), calls=%async_computation.21 | async-start | bytes 7520256 | tf_op jit(solution)/shard_map/all_to_all | solution.py:637
  1369.2 58.3 %all-to-all-start.20 = ((bf16[4,408,1088]{2,1,0:T(8,128)(2,1)}), bf16[4,408,1088]{2,1,0:T(8,128)(2,1)}, u32[]{:S(2)}, u32[]{:S(2)}) async-start(bf16[4,408,1088]{2,1,0:T(8,128)(2,1)} %broadcast_in_dim.43), calls=%async_computation.26 | async-start | bytes 7520256 | tf_op jit(solution)/shard_map/all_to_all | solution.py:637
  (143 other events, 3284.2 us)
Sparse Core Ops, SparseCore 0:
  9.7 48.9 all-gather.15
  60.8 89.6 all-gather.17
  152.8 94.0 all-gather.19
  248.9 70.9 all-gather.13
  321.4 31.4 all-gather.21
  354.5 90.0 all-gather.23
  446.8 94.0 all-gather.25
  574.0 144.3 reduce-scatter.6
  720.7 98.4 reduce-scatter.8
  838.6 99.2 all-reduce.3
  940.2 100.2 reduce-scatter.10
  1042.7 103.4 reduce-scatter.12
  1148.4 98.4 reduce-scatter.14
  1264.9 98.4 reduce-scatter.16

commit v2 on v1

--- a/solution.py
+++ b/solution.py
@@ -175,12 +175,14 @@
       )(inv,nb,x,o,do,lse)
 
 
-def one_fwd_kernel(own_ref, q_ref, x_ref, o_ref, lse_ref, vt, sb, acc, *, B, NB):
+def one_fwd_kernel(own_ref, q_ref, x_ref, o_ref, lse_ref, vt, kd, acc, *, B, NB):
     nb = own_ref[NB + 2]
+    low = lax.broadcasted_iota(jnp.int32,(1,128),1)<64
     def tv(j,_):
         r=pl.multiple_of(own_ref[j]*B,B)
         t=x_ref[pl.ds(r,B),:].T
         w=pl.multiple_of(j*B,B)
+        kd[pl.ds(w,B),:]=dup(x_ref[pl.ds(r,B),:],0,low)
         vt[0:64,pl.ds(w,B)]=t[64:128,:]
         vt[64:80,pl.ds(w,B)]=(lax.broadcasted_iota(jnp.int32,(16,B),0)==0).astype(bf16)
         return 0
@@ -196,12 +198,11 @@
         @pl.when(i<nb)
         def _():
             qs=q_ref[t*B:(t+1)*B,:].astype(f32)*(0.125*LOG2E)
-            q=qs.astype(bf16)
-            ql=(qs-q.astype(f32)).astype(bf16)
+            hi=qs.astype(bf16)
+            q=jnp.concatenate([hi.astype(f32),qs-hi.astype(f32)],axis=1).astype(bf16)
             acc[...]=jnp.zeros_like(acc)
             def step(j,m,diag):
-                k=x_ref[pl.ds(pl.multiple_of(own_ref[j]*B,B),B),0:64]
-                st=dot_nt(k,q)+dot_nt(k,ql)
+                st=dot_nt(kd[pl.ds(pl.multiple_of(j*B,B),B),:],q)
                 if diag: st=jnp.where(rr<=cc,st,NEG)
                 mn=jnp.maximum(m,jnp.max(st,axis=0,keepdims=True))
                 p=jnp.exp2(st-mn)
@@ -225,7 +226,7 @@
       grid_spec=pltpu.PrefetchScalarGridSpec(num_scalar_prefetch=1,grid=(1,),
         in_specs=[pl.BlockSpec((R,64),full),pl.BlockSpec((N,128),last)],
         out_specs=[pl.BlockSpec((R,64),full),pl.BlockSpec((8,R),full)],
-        scratch_shapes=[pltpu.VMEM((80,N),bf16),pltpu.VMEM((B,B),f32),pltpu.VMEM((80,B),f32)]),
+        scratch_shapes=[pltpu.VMEM((80,N),bf16),pltpu.VMEM((N,128),bf16),pltpu.VMEM((80,B),f32)]),
       compiler_params=pltpu.CompilerParams(vmem_limit_bytes=48<<20),
       cost_estimate=pl.CostEstimate(flops=4*R*N*128,bytes_accessed=N*256+R*512,transcendentals=R*N),
       )(own,q,x)
@@ -233,6 +234,7 @@
 
 def one_bwd_kernel(own_ref, q_ref, x_ref, o_ref, do_ref, lse_ref, dq_ref, dx_ref, dkv, dq, *, B, NB):
     nb = own_ref[NB + 2]
+    low = lax.broadcasted_iota(jnp.int32,(1,128),1)<64
     rr=lax.broadcasted_iota(jnp.int32,(B,B),0)
     cc=lax.broadcasted_iota(jnp.int32,(B,B),1)
     ones=jnp.ones((8,64),bf16)
@@ -247,8 +249,8 @@
         def _():
             qr=q_ref[sl,:]
             qs=qr.astype(f32)*(0.125*LOG2E)
-            q=qs.astype(bf16)
-            ql=(qs-q.astype(f32)).astype(bf16)
+            hi=qs.astype(bf16)
+            q=jnp.concatenate([hi.astype(f32),qs-hi.astype(f32)],axis=1).astype(bf16)
             qd=qr*jnp.asarray(0.125,bf16)
             do=do_ref[sl,:]
             prod=o_ref[sl,:].astype(f32)*do.astype(f32)
@@ -260,7 +262,7 @@
                 r=pl.multiple_of(own_ref[j]*B,B)
                 k=x_ref[pl.ds(r,B),0:64]
                 v=x_ref[pl.ds(r,B),64:128]
-                st=dot_nt(k,q)+dot_nt(k,ql)
+                st=dot_nt(dup(x_ref[pl.ds(r,B),:],0,low),q)
                 p=jnp.exp2(st-lse)
                 if diag: p=jnp.where(rr<=cc,p,0.0)
                 dp=dot_nt(v,do)
@@ -678,7 +680,7 @@
         u = jnp.dot(n2, up_w, preferred_element_type=f32) + vector(8, layer)
         a, slope = gelu_parts(u)
         a = a.astype(bf16)
-        slope = slope.astype(bf16)
+        a, slope = after(a, slope.astype(bf16))
         records.append((stream, n1, heads, q16, o, lse, o16, lse16, mixed, m, n2, a, slope))
         stream = m + jnp.dot(a, down_w, preferred_element_type=f32) + vector(7, layer)
     activations = (stream * live).astype(bf16)[None]
@@ -746,6 +748,8 @@
         gmb = gm.astype(bf16)
         d_out_b = col_sum(gmb)
         d_out = jnp.einsum("rd,re->de", mixed, gmb, preferred_element_type=f32).astype(bf16)
+        if layer == 0:
+            gmb, d_out = after(gmb, plain(d_out))
         if layer < L - 1:
             done = after(gmb, *ffn_sum)
             gmb, ffn_sum = done[0], done[1:]
@@ -788,10 +792,12 @@
             d_back, mine = after(d_row, mine)
             middle = ctx_end(mine)
         d_qkv = jnp.einsum("rd,rc->dc", n1, d_row, preferred_element_type=f32).astype(bf16)
-        d_four = jnp.concatenate([d_qkv, d_out], axis=1)
         if layer:
-            d_row, d_four = after(d_row, plain(d_four))
-        d_four = reduce_fsdp(d_four)
+            d_row, d_four = after(d_row, plain(jnp.concatenate([d_qkv, d_out], axis=1)))
+            d_four = reduce_fsdp(d_four)
+        else:
+            d_qkv, d_out = after(d_qkv, reduce_fsdp(d_out))
+            d_four = jnp.concatenate([reduce_fsdp(d_qkv), d_out], axis=1)
         sums = unpack(col_sum(d_row)[None])[0]
         dn1 = jnp.einsum("rc,dc->rd", d_back, qkv_w, preferred_element_type=f32)
         back, d_gain1, d_bias1 = norm_back(dn1, stream_in, vector(0, layer))
@@ -800,17 +806,18 @@
         ffns[layer] = (d_up, d_down)
         if layer == 0:
             last = ctx_sum([d_four])
-            rest = spread((middle, middle_sizes), [wide_shape, wide_shape, tall_shape])
-            matrices[1] = [rest[0], ffn_sum[0].astype(f32), ffn_sum[1].astype(f32)]
-            matrices[0] = spread(last, [wide_shape]) + rest[1:]
         small[layer] = jnp.concatenate([
             t.reshape(-1, n) for t, n in (
                 (d_gain1, shard), (d_bias1, shard), (sums[:width], shard), (sums[2 * width:], shard), (d_out_b, shard),
                 (d_gain2, shard), (d_bias2, shard), (d_down_b, shard), (d_up_b, 4 * shard))], axis=1)
 
     vec_grads = jnp.stack(small, axis=1)
+    vec_grads, middle, activations = after(vec_grads, middle, activations)
     vec_grads = jnp.sum(lax.all_to_all(vec_grads, FS, 0, 0), axis=0)
-    vec_grads = lax.psum(vec_grads, "ctx")
+    vec_grads = jnp.sum(lax.all_to_all(jnp.broadcast_to(vec_grads[None], (C,) + vec_grads.shape), "ctx", 0, 0), axis=0)
+    rest = spread((middle, middle_sizes), [wide_shape, wide_shape, tall_shape])
+    matrices[1] = [rest[0], ffn_sum[0].astype(f32), ffn_sum[1].astype(f32)]
+    matrices[0] = spread(last, [wide_shape]) + rest[1:]
     vg = [vec_grads[:, i * shard:(i + 1) * shard] for i in range(8)] + [vec_grads[:, 8 * shard:]]
 
     g_qkv = jnp.stack([unpack(matrices[layer][0][:, :3 * width]) for layer in range(L)])

time: 1530 us -> 1550 us (1.013); the launches traced: 1510 us -> 1550 us
  Pallas kernels: 279 us -> 473 us
  waiting for transfers between devices: 472 us -> 361 us
  blocking collectives: 38.2 us -> 0 us
    pallas_call x4, Pallas kernels: 97.5 us -> 206 us  [flash_bwd(): pl.pallas_call(functools.partial(bwd_kernel, B=B, NB=NB), out_shape=jax.S...]
    pallas_call x4, Pallas kernels: 63 us -> 136 us  [flash_fwd(): pl.pallas_call(functools.partial(fwd_kernel, B=B, NB=NB), out_shape=(jax....]
    reduce_scatter x6, waiting for transfers between devices: 141 us -> 68 us  [reduce_fsdp(): return lax.psum_scatter(g.astype(bf16), FS, scatter_dimension=0, tiled=True)]
    all_to_all x20, waiting for transfers between devices: 313 us -> 249 us  [exchange(): return plain(lax.all_to_all(plain(x), 'ctx', 0, 0))]
    psum x1 -> x0, blocking collectives: 27.5 us -> none  [local(): vec_grads = lax.psum(vec_grads, 'ctx')]
    optimization_barrier x0 -> x1, waiting for transfers between devices: none -> 25.8 us  [after(): return lax.optimization_barrier((x,) + others)]
    dot_general x2, matrix products: 59.3 us -> 38.3 us  [local(): jnp.einsum('rd,fd->rf', gb, down_w, preferred_element_type=f32)]
  transfers between devices with their start and end apart: 43 -> 46, of which waited for: 23 -> 23; matrix products, arithmetic and copies ran while one was open for 36% -> 36% of each run, Pallas kernels for 18% -> 30%
where the time goes in v2:
time: 1550 us
  Pallas kernels  473 us (31%)
  matrix products  411 us (27%)
  waiting for transfers between devices  361 us (23%)
  starting transfers between devices  102 us (7%)
  local copies, waits for them, and re-layouts  97.9 us (6%)
  other arithmetic  92.9 us (6%)
  between operations  17.5 us (1%)
    all_to_all x20, waiting for transfers between devices, exchange(): return plain(lax.all_to_all(plain(x), 'ctx', 0, 0))  249 us
    pallas_call x4, Pallas kernels, flash_bwd(): pl.pallas_call(functools.partial(bwd_kernel, B=B, NB=NB), out_shape=jax.S...  206 us
    pallas_call x4, Pallas kernels, flash_fwd(): pl.pallas_call(functools.partial(fwd_kernel, B=B, NB=NB), out_shape=(jax....  136 us
    all_to_all x20, starting transfers between devices, exchange(): return plain(lax.all_to_all(plain(x), 'ctx', 0, 0))  90 us
    dot_general x2, matrix products, local(): u = jnp.dot(n2, up_w, preferred_element_type=f32) + vector(8, layer)  82.6 us
    reduce_scatter x6, waiting for transfers between devices, reduce_fsdp(): return lax.psum_scatter(g.astype(bf16), FS, scatter_dimension=0, tiled=True)  68 us
    pallas_call x1, Pallas kernels, gather_all(): pl.pallas_call(functools.partial(gather_kernel, Z=Z, C=C, quarter=W // C)...  54.5 us
    dot_general x2, matrix products, local(): dn2 = jnp.einsum('rf,df->rd', du, up_w, preferred_element_type=f32)  39 us
  transfers between devices with their start and end apart: 46, of which 23 were waited for; matrix products, arithmetic and copies ran while one was open for 36% of the time, Pallas kernels for 30%

profile of v2, /device:TPU:0, one launch (start us, length us, event | category | flops | bytes accessed | tf_op | source)
XLA Modules:
  0.0 1554.4 jit_solution(9611764375981415552)
XLA Ops:
  30.9 54.5 %shard_map.280 = bf16[8,136,3584]{2,1,0:T(8,128)(2,1)} custom-call(bf16[136,3584]{1,0:T(8,128)(2,1)} %pad.4.x_ref), custom_call_target="tpu_custom_call" | custom-call | bytes 38993920 | tf_op jit(solution)/shard_map/pallas_call | solution.py:512
  128.3 31.4 %all-to-all-done = bf16[4,1024,384]{2,1,0:T(8,128)(2,1)S(1)} async-done(((bf16[4,1024,384]{2,1,0:T(8,128)(2,1)}), bf16[4,1024,384]{2,1,0:T(8,128)(2,1)S(1)}, u32[]{:S(2)}, u32[]{:S(2)}) %all-to-all-start) | async-done | bytes 3145760 | tf_op jit(solution)/shard_map/all_to_all | solution.py:639
  167.4 24.6 %shard_map.284 = (bf16[1,4096,128]{2,1,0:T(8,128)(2,1)S(1)}, f32[1,8,4096]{2,1,0:T(8,128)S(1)}) custom-call(s32[1,8]{1,0:T(1,128)S(1)} %bitcast.289, s32[1]{0:T(128)S(6)} %select_n.21.nb_ref, bf16[1,4096,384]{2,1,0:T(8,128)(2,1)S(1)} %bitcast.277), custom_call_target="tpu_custom_call" | custom-call | flops 8589934592 | bytes 4194304 | tf_op jit(solution)/shard_map/pallas_call | solution.py:88
  215.5 43.3 %shard_map.283 = (bf16[1,4096,128]{2,1,0:T(8,128)(2,1)S(1)}, f32[1,8,4096]{2,1,0:T(8,128)S(1)}) custom-call(s32[1,8]{1,0:T(1,128)S(1)} %slice_bitcast_fusion.9.inv_ref, s32[1]{0:T(128)} %slice.941.nb_ref, bf16[1,4096,512]{2,1,0:T(8,128)(2,1)} %bitcast.18.x_ref), custom_call_target="tpu_custom_call" | custom-call | flops 8589934592 | bytes 4194304 | tf_op jit(solution)/shard_map/pallas_call | solution.py:88
  296.1 46.3 %add_convert_fusion.1 = (bf16[1024,4352]{1,0:T(8,128)(2,1)}, bf16[1024,4352]{1,0:T(8,128)(2,1)}) fusion(f32[4352]{0:T(1024)S(1)} %add.288, bf16[1,1088,4352]{2,1,0:T(8,128)(2,1)} %all-gather.18.cloned.1.call-done, f32[1024,1088]{0,1:T(8,128)} %copy-done.51, f32[1088]{0:T(1024)S(1)} %copy-done.99, f32[1088]{0:T(1024)S(1)} %get-tuple-element.177, ...), kind=kOutput, calls=%fused_computation.14 | convolution fusion | flops 9827581952 | bytes 31786496 | tf_op jit(solution)/shard_map/dot_general | solution.py:680
  397.3 30.8 %all-to-all-done.4 = bf16[4,1024,384]{2,1,0:T(8,128)(2,1)S(1)} async-done(((bf16[4,1024,384]{2,1,0:T(8,128)(2,1)}), bf16[4,1024,384]{2,1,0:T(8,128)(2,1)S(1)}, u32[]{:S(2)}, u32[]{:S(2)}) %all-to-all-start.4) | async-done | bytes 3145760 | tf_op jit(solution)/shard_map/all_to_all | solution.py:639
  433.0 24.5 %shard_map.290 = (bf16[1,4096,128]{2,1,0:T(8,128)(2,1)S(1)}, f32[1,8,4096]{2,1,0:T(8,128)S(1)}) custom-call(s32[1,8]{1,0:T(1,128)S(1)} %bitcast.290, s32[1]{0:T(128)S(6)} %select_n.21.nb_ref, bf16[1,4096,384]{2,1,0:T(8,128)(2,1)S(1)} %bitcast.279), custom_call_target="tpu_custom_call" | custom-call | flops 8589934592 | bytes 4194304 | tf_op jit(solution)/shard_map/pallas_call | solution.py:88
  459.2 21.5 %all-to-all-done.5 = bf16[4,1024,512]{2,1,0:T(8,128)(2,1)} async-done(((bf16[4,1024,512]{2,1,0:T(8,128)(2,1)}), bf16[4,1024,512]{2,1,0:T(8,128)(2,1)}, u32[]{:S(2)}, u32[]{:S(2)}) %all-to-all-start.5) | async-done | bytes 4194336 | tf_op jit(solution)/shard_map/all_to_all | solution.py:639
  484.3 43.4 %shard_map.289 = (bf16[1,4096,128]{2,1,0:T(8,128)(2,1)S(1)}, f32[1,8,4096]{2,1,0:T(8,128)S(1)}) custom-call(s32[1,8]{1,0:T(1,128)S(1)} %slice_bitcast_fusion.9.inv_ref, s32[1]{0:T(128)} %slice.941.nb_ref, bf16[1,4096,512]{2,1,0:T(8,128)(2,1)} %bitcast.32.x_ref), custom_call_target="tpu_custom_call" | custom-call | flops 8589934592 | bytes 4194304 | tf_op jit(solution)/shard_map/pallas_call | solution.py:88
  565.3 36.3 %add_convert_fusion = (bf16[1024,4352]{1,0:T(8,128)(2,1)}, bf16[1024,4352]{1,0:T(8,128)(2,1)}) fusion(f32[4352]{0:T(1024)S(1)} %add.316, bf16[1,1088,4352]{2,1,0:T(8,128)(2,1)} %all-gather.24.cloned.1.call-done, f32[1024,1088]{0,1:T(8,128)} %copy-done.39, f32[1088]{0:T(1024)S(1)} %copy-done.103, f32[1088]{0:T(1024)S(1)} %copy-done.72, ...), kind=kOutput, calls=%fused_computation.12 | convolution fusion | flops 9827581952 | bytes 31786496 | tf_op jit(solution)/shard_map/dot_general | solution.py:680
  619.3 19.8 %multiply_convert_fusion.1 = bf16[1024,4352]{1,0:T(8,128)(2,1)} fusion(bf16[1024,4352]{1,0:T(8,128)(2,1)} %get-tuple-element.100, bf16[1024,1088]{0,1:T(8,128)(2,1)} %fusion.55, bf16[1,4352,1088]{2,1,0:T(8,128)(2,1)} %all-gather.26.cloned.1.call-done), kind=kOutput, calls=%fused_computation.11 | convolution fusion | flops 9710600192 | bytes 29523968 | tf_op jit(solution)/shard_map/rd,fd->rf/dot_general | solution.py:740
  658.4 19.4 %multiply_reduce_fusion = (f32[1088]{0:T(1024)}, f32[1024]{0:T(1024)S(1)}, f32[1024]{0:T(1024)S(1)}, f32[1088]{0:T(1024)}, f32[1024,1088]{0,1:T(8,128)S(1)}) fusion(f32[1024,1088]{0,1:T(8,128)} %copy-done.39, f32[1024]{0:T(1024)S(1)} %add_rsqrt_fusion, f32[1024]{0:T(1024)S(1)} %broadcast_multiply_fusion.8, f32[1088]{0:T(1024)S(1)} %copy-done.72, ...), kind=kOutput, calls=%fused_computation.72 | convolution fusion | flops 9707253760 | bytes 27325184 | tf_op jit(solution)/shard_map/rf,df->rd/dot_general | solution.py:745
  714.9 38.0 %shard_map.295 = bf16[1,4096,384]{2,1,0:T(8,128)(2,1)S(1)} custom-call(s32[1,8]{1,0:T(1,128)S(1)} %bitcast.291, s32[1]{0:T(128)S(6)} %select_n.21.nb_ref, bf16[1,4096,384]{2,1,0:T(8,128)(2,1)} %bitcast.280, bf16[1,4096,128]{2,1,0:T(8,128)(2,1)S(1)} %copy-done.7, bf16[1,4096,128]{2,1,0:T(8,128)(2,1)S(1)} %bitcast.286, f32[1,8,4096]{2,1,0:T(8,128)S(1)} %copy-done.38), custom_call_target="tpu_custom_call" | custom-call | flops 21474836480 | bytes 9830400 | tf_op jit(solution)/shard_map/pallas_call | solution.py:166
  760.3 64.6 %shard_map.294 = bf16[1,4096,384]{2,1,0:T(8,128)(2,1)} custom-call(s32[1,8]{1,0:T(1,128)S(1)} %copy-done.30, s32[1]{0:T(128)} %slice.941.nb_ref, bf16[1,4096,512]{2,1,0:T(8,128)(2,1)} %bitcast.32.x_ref, bf16[1,4096,128]{2,1,0:T(8,128)(2,1)S(1)} %copy-done.28, bf16[1,4096,256]{2,1,0:T(8,128)(2,1)S(1)} %bitcast.276, f32[1,8,4096]{2,1,0:T(8,128)S(1)} %copy-done.34), custom_call_target="tpu_custom_call" | custom-call | flops 21474836480 | bytes 9830400 | tf_op jit(solution)/shard_map/pallas_call | solution.py:166
  844.6 28.5 %all-to-all-done.11.refs_1_ = bf16[4,1024,384]{2,1,0:T(8,128)(2,1)} async-done(((bf16[4,1024,384]{2,1,0:T(8,128)(2,1)}), bf16[4,1024,384]{2,1,0:T(8,128)(2,1)}, u32[]{:S(2)}, u32[]{:S(2)}) %all-to-all-start.11) | async-done | bytes 3145760 | tf_op jit(solution)/shard_map/all_to_all | solution.py:639
  980.4 19.6 %multiply_reduce_fusion.2 = (f32[1088]{0:T(1024)}, f32[1024]{0:T(1024)S(1)}, f32[1024]{0:T(1024)S(1)}, f32[1088]{0:T(1024)S(1)}, f32[1024,1088]{0,1:T(8,128)S(1)}) fusion(f32[1024,1088]{0,1:T(8,128)} %copy-done.51, f32[1024]{0:T(1024)S(1)} %copy-done.95, f32[1024]{0:T(1024)S(1)} %copy-done.81, f32[1088]{0:T(1024)S(1)} %copy-done.87, ...), kind=kOutput, calls=%fused_computation.74 | convolution fusion | flops 9707253760 | bytes 27325184 | tf_op jit(solution)/shard_map/rf,df->rd/dot_general | solution.py:745
  1036.0 32.6 %reduce-scatter.14.cloned.1.call-done = bf16[136,4352]{1,0:T(8,128)(2,1)} async-done(((bf16[1088,4352]{1,0:T(8,128)(2,1)}), bf16[136,4352]{1,0:T(8,128)(2,1)}) %reduce-scatter.14.cloned.1.call-update) | async-done | bytes 1183760 | tf_op jit(solution)/shard_map/reduce_scatter | solution.py:689
  1073.4 38.9 %shard_map.299 = bf16[1,4096,384]{2,1,0:T(8,128)(2,1)S(1)} custom-call(s32[1,8]{1,0:T(1,128)S(1)} %bitcast.292, s32[1]{0:T(128)S(6)} %select_n.21.nb_ref, bf16[1,4096,384]{2,1,0:T(8,128)(2,1)} %bitcast.278, bf16[1,4096,128]{2,1,0:T(8,128)(2,1)S(1)} %copy-done.5, bf16[1,4096,128]{2,1,0:T(8,128)(2,1)S(1)} %bitcast.285, f32[1,8,4096]{2,1,0:T(8,128)S(1)} %copy-done.36), custom_call_target="tpu_custom_call" | custom-call | flops 21474836480 | bytes 9830400 | tf_op jit(solution)/shard_map/pallas_call | solution.py:166
  1118.8 64.6 %shard_map.298 = bf16[1,4096,384]{2,1,0:T(8,128)(2,1)} custom-call(s32[1,8]{1,0:T(1,128)S(1)} %copy-done.30, s32[1]{0:T(128)} %slice.941.nb_ref, bf16[1,4096,512]{2,1,0:T(8,128)(2,1)} %bitcast.18.x_ref, bf16[1,4096,128]{2,1,0:T(8,128)(2,1)S(1)} %copy-done.26, bf16[1,4096,256]{2,1,0:T(8,128)(2,1)S(1)} %bitcast.275, f32[1,8,4096]{2,1,0:T(8,128)S(1)} %copy-done.32), custom_call_target="tpu_custom_call" | custom-call | flops 21474836480 | bytes 9830400 | tf_op jit(solution)/shard_map/pallas_call | solution.py:166
  1197.9 33.2 %all-to-all-done.15.refs_1_ = bf16[4,1024,384]{2,1,0:T(8,128)(2,1)} async-done(((bf16[4,1024,384]{2,1,0:T(8,128)(2,1)}), bf16[4,1024,384]{2,1,0:T(8,128)(2,1)}, u32[]{:S(2)}, u32[]{:S(2)}) %all-to-all-start.15) | async-done | bytes 3145760 | tf_op jit(solution)/shard_map/all_to_all | solution.py:639
  1239.9 35.0 %reduce-scatter.18.cloned.1.call-done = bf16[136,4352]{1,0:T(8,128)(2,1)} async-done(((bf16[1088,4352]{1,0:T(8,128)(2,1)}), bf16[136,4352]{1,0:T(8,128)(2,1)}) %reduce-scatter.18.cloned.1.call-update) | async-done | bytes 1183760 | tf_op jit(solution)/shard_map/reduce_scatter | solution.py:689
  1288.1 25.8 %reduce-scatter.22.cloned.1.call-done = bf16[136,1088]{1,0:T(8,128)(2,1)} async-done(((bf16[1088,1088]{1,0:T(8,128)(2,1)}), bf16[136,1088]{1,0:T(8,128)(2,1)}) %reduce-scatter.22.cloned.1.call-update) | async-done | bytes 295952 | tf_op jit(solution)/shard_map/optimization_barrier | solution.py:642
  1367.4 34.9 %all-to-all-done.16 = bf16[4,408,1088]{2,1,0:T(8,128)(2,1)} async-done(((bf16[4,408,1088]{2,1,0:T(8,128)(2,1)}), bf16[4,408,1088]{2,1,0:T(8,128)(2,1)}, u32[]{:S(2)}, u32[]{:S(2)}) %all-to-all-start.16) | async-done | bytes 3551264 | tf_op jit(solution)/shard_map/all_to_all | solution.py:639
  1435.5 19.5 %all-to-all-done.17 = bf16[4,408,1088]{2,1,0:T(8,128)(2,1)} async-done(((bf16[4,408,1088]{2,1,0:T(8,128)(2,1)}), bf16[4,408,1088]{2,1,0:T(8,128)(2,1)}, u32[]{:S(2)}, u32[]{:S(2)}) %all-to-all-start.17) | async-done | bytes 3551264 | tf_op jit(solution)/shard_map/all_to_all | solution.py:639
  (600 shorter events, 705.8 us)
Async XLA Ops:
  7.2 280.3 %all-gather.16.cloned.1.call-start = ((), (), s32[]{:S(2)}) async-start(), calls=%async_computation.36 | async-start | bytes 2820096 | tf_op jit(solution)/shard_map/all_gather | solution.py:605
  9.5 286.6 %all-gather.18.cloned.1.call-start = ((), (), s32[]{:S(2)}) async-start(), calls=%async_computation.37 | async-start | bytes 10653696 | tf_op jit(solution)/shard_map/all_gather | solution.py:605
  13.7 328.8 %all-gather.20.cloned.1.call-start = ((), (), s32[]{:S(2)}) async-start(), calls=%async_computation.38 | async-start | bytes 11280384 | tf_op jit(solution)/shard_map/all_gather | solution.py:605
  18.1 345.6 %all-gather.14.cloned.1.call-start = ((), (), s32[]{:S(2)}) async-start(), calls=%async_computation.29 | async-start | bytes 8146944 | tf_op jit(solution)/shard_map/all_gather | solution.py:605
  123.2 432.3 %all-gather.22.cloned.1.call-start = ((), (), s32[]{:S(2)}) async-start(), calls=%async_computation.39 | async-start | bytes 2820096 | tf_op jit(solution)/shard_map/all_gather | solution.py:605
  159.8 52.2 %all-to-all-start.1 = ((bf16[4,1024,512]{2,1,0:T(8,128)(2,1)}), bf16[4,1024,512]{2,1,0:T(8,128)(2,1)}, u32[]{:S(2)}, u32[]{:S(2)}) async-start(bf16[4,1024,512]{2,1,0:T(8,128)(2,1)} %pad_maximum_fusion.1), calls=%async_computation.1 | async-start | bytes 8388608 | tf_op jit(solution)/shard_map/all_to_all | solution.py:639
  164.7 400.5 %all-gather.24.cloned.1.call-start = ((), (), s32[]{:S(2)}) async-start(), calls=%async_computation.40 | async-start | bytes 10653696 | tf_op jit(solution)/shard_map/all_gather | solution.py:605
  212.0 47.5 %all-to-all-start.2 = ((bf16[4,1024,128]{2,1,0:T(8,128)(2,1)}), bf16[4,1024,128]{2,1,0:T(8,128)(2,1)S(1)}, u32[]{:S(2)}, u32[]{:S(2)}) async-start(bf16[4,1024,128]{2,1,0:T(8,128)(2,1)} %bitcast.283), calls=%async_computation.2 | async-start | bytes 2097152 | tf_op jit(solution)/shard_map/all_to_all | solution.py:639
  391.1 228.3 %all-gather.26.cloned.1.call-start = ((), (), s32[]{:S(2)}) async-start(), calls=%async_computation.41 | async-start | bytes 11280384 | tf_op jit(solution)/shard_map/all_gather | solution.py:605
  428.1 52.6 %all-to-all-start.5 = ((bf16[4,1024,512]{2,1,0:T(8,128)(2,1)}), bf16[4,1024,512]{2,1,0:T(8,128)(2,1)}, u32[]{:S(2)}, u32[]{:S(2)}) async-start(bf16[4,1024,512]{2,1,0:T(8,128)(2,1)} %pad_maximum_fusion.2), calls=%async_computation.5 | async-start | bytes 8388608 | tf_op jit(solution)/shard_map/all_to_all | solution.py:639
  480.7 47.0 %all-to-all-start.6 = ((bf16[4,1024,128]{2,1,0:T(8,128)(2,1)}), bf16[4,1024,128]{2,1,0:T(8,128)(2,1)S(1)}, u32[]{:S(2)}, u32[]{:S(2)}) async-start(bf16[4,1024,128]{2,1,0:T(8,128)(2,1)} %bitcast.284), calls=%async_computation.6 | async-start | bytes 2097152 | tf_op jit(solution)/shard_map/all_to_all | solution.py:639
  534.8 290.1 %reduce-scatter.10.cloned.1.call-start = ((), (), s32[]{:S(2)}) async-start(), calls=%async_computation.30 | async-start | bytes 11280384 | tf_op jit(solution)/shard_map/reduce_scatter | solution.py:689
  619.3 206.0 %reduce-scatter.12.cloned.1.call-start = ((), (), s32[]{:S(2)}) async-start(), calls=%async_computation.31 | async-start | bytes 10653696 | tf_op jit(solution)/shard_map/reduce_scatter | solution.py:689
  706.1 48.5 %all-to-all-start.9 = ((bf16[4,1024,256]{2,1,0:T(8,128)(2,1)}), bf16[4,1024,256]{2,1,0:T(8,128)(2,1)S(1)}, u32[]{:S(2)}, u32[]{:S(2)}) async-start(bf16[4,1024,256]{2,1,0:T(8,128)(2,1)} %pad_maximum_fusion.5), calls=%async_computation.9 | async-start | bytes 4194304 | tf_op jit(solution)/shard_map/all_to_all | solution.py:639
  754.6 70.3 %all-to-all-start.10 = ((bf16[4,1024,384]{2,1,0:T(8,128)(2,1)}), bf16[4,1024,384]{2,1,0:T(8,128)(2,1)}, u32[]{:S(2)}, u32[]{:S(2)}) async-start(bf16[4,1024,384]{2,1,0:T(8,128)(2,1)} %bitcast.282), calls=%async_computation.10 | async-start | bytes 6291456 | tf_op jit(solution)/shard_map/all_to_all | solution.py:639
  835.9 174.3 %all-reduce.5.cloned.1.call-start = ((), (), s32[]{:S(2)}) async-start(), calls=%async_computation.43 | async-start | bytes 4874240 | tf_op jit(solution)/shard_map/psum | solution.py:784
  844.1 224.4 %reduce-scatter.14.cloned.1.call-start = ((), (), s32[]{:S(2)}) async-start(), calls=%async_computation.32 | async-start | bytes 10653696 | tf_op jit(solution)/shard_map/reduce_scatter | solution.py:689
  900.5 283.0 %reduce-scatter.16.cloned.1.call-start = ((), (), s32[]{:S(2)}) async-start(), calls=%async_computation.33 | async-start | bytes 11280384 | tf_op jit(solution)/shard_map/reduce_scatter | solution.py:689
  940.1 334.8 %reduce-scatter.18.cloned.1.call-start = ((), (), s32[]{:S(2)}) async-start(), calls=%async_computation.34 | async-start | bytes 10653696 | tf_op jit(solution)/shard_map/reduce_scatter | solution.py:689
  1068.5 45.4 %all-to-all-start.13 = ((bf16[4,1024,256]{2,1,0:T(8,128)(2,1)}), bf16[4,1024,256]{2,1,0:T(8,128)(2,1)S(1)}, u32[]{:S(2)}, u32[]{:S(2)}) async-start(bf16[4,1024,256]{2,1,0:T(8,128)(2,1)} %pad_maximum_fusion.6), calls=%async_computation.16 | async-start | bytes 4194304 | tf_op jit(solution)/shard_map/all_to_all | solution.py:639
  1113.9 69.5 %all-to-all-start.14 = ((bf16[4,1024,384]{2,1,0:T(8,128)(2,1)}), bf16[4,1024,384]{2,1,0:T(8,128)(2,1)}, u32[]{:S(2)}, u32[]{:S(2)}) async-start(bf16[4,1024,384]{2,1,0:T(8,128)(2,1)} %bitcast.281), calls=%async_computation.17 | async-start | bytes 6291456 | tf_op jit(solution)/shard_map/all_to_all | solution.py:639
  1118.7 195.1 %reduce-scatter.22.cloned.1.call-start = ((), (), s32[]{:S(2)}) async-start(), calls=%async_computation.42 | async-start | bytes 2820096
  1194.1 276.7 %reduce-scatter.20.cloned.1.call-start = ((), (), s32[]{:S(2)}) async-start(), calls=%async_computation.35 | async-start | bytes 8146944 | tf_op jit(solution)/shard_map/reduce_scatter | solution.py:689
  1407.7 47.3 %all-to-all-start.17 = ((bf16[4,408,1088]{2,1,0:T(8,128)(2,1)}), bf16[4,408,1088]{2,1,0:T(8,128)(2,1)}, u32[]{:S(2)}, u32[]{:S(2)}) async-start(bf16[4,408,1088]{2,1,0:T(8,128)(2,1)} %broadcast_in_dim.45), calls=%async_computation.22 | async-start | bytes 7520256 | tf_op jit(solution)/shard_map/all_to_all | solution.py:639
  (152 other events, 3711.1 us)
Sparse Core Ops, SparseCore 0:
  9.7 48.8 all-gather.15
  60.8 89.6 all-gather.17
  152.7 94.0 all-gather.19
  248.9 70.9 all-gather.13
  321.4 31.4 all-gather.21
  354.4 90.0 all-gather.23
  446.7 94.0 all-gather.25
  619.4 105.0 reduce-scatter.9
  726.8 98.4 reduce-scatter.11
  844.2 121.6 all-reduce.4
  968.2 100.2 reduce-scatter.13
  1070.7 103.4 reduce-scatter.15
  1176.5 98.4 reduce-scatter.17
  1277.1 36.7 reduce-scatter.21
  1316.2 78.1 reduce-scatter.19
